TPU v7x, 32 devices: a whole 2x2x4 slice. The times are simulated.
32 devices in a mesh: grp: 2 (over x), tp: 16 (over z, y, core).
Axes of the slice: x: 2, y: 2, z: 4, core: 2. Of those that a mesh axis runs over, the one named last changes fastest.
Arguments:
- residual_input: bfloat16 [256, 5120], P('grp', 'tp'), may hold values from -6 to 6
- input_norm_gain: float32 [5120], replicated, may hold values from 0.1 to 1.9
- query_weight: bfloat16 [5120, 4096], P(None, 'tp'), may hold values from -0.078125 to 0.078125
- key_value_weight: bfloat16 [5120, 1024], P(None, 'tp'), may hold values from -0.3125 to 0.3125
- shared_down_factors: bfloat16 [5120, 48], replicated, may hold values from -0.078125 to 0.078125
- query_up_factors: bfloat16 [16, 16, 4096], P(None, None, 'tp'), may hold values from -1 to 1
- key_value_up_factors: bfloat16 [16, 16, 1024], replicated, may hold values from -1 to 1
- paged_base_keys: bfloat16 [128, 128, 512], P(('grp', 'tp')), may hold values from -100 to 100
- paged_base_values: bfloat16 [128, 128, 512], P(('grp', 'tp')), may hold values from -6 to 6
- paged_down_factors: bfloat16 [128, 128, 32], P(('grp', 'tp')), may hold values from -6 to 6
- adapter_of_row: int32 [256], P('grp'), may hold values from 0 to 15
- document_of_row: int32 [256, 1], P('grp'), may hold values from 0 to 1; in each aligned block of 128 rows (0 to 127, 128 to 255, ...) at most 128 rows name the same one
- document_page_slots: int32 [2, 64], replicated, may hold values from 0 to 127, as said below
Outputs:
- attended: bfloat16 [256, 4096], P('grp', 'tp')
Inputs may be any that keep to these rules, and one draw needn't show every extreme that they name: `document_of_row`: in each aligned block of 128 rows no document is named by more than 128 rows. `document_page_slots`: each page slot is used once; all pages of one document lie on the 16 devices of one index of grp, 4 on each, documents and indices of grp one to one.
All inputs are finite; a program needn't handle non-finite values.
Results may differ from a plain program's by a relative error of at most 0.034.
Values may be sent and summed in bfloat16 or wider, within the bound.
A program may use at most 64 MiB of HBM per device.

v0:
```python
import jax
import jax.numpy as jnp
from jax import lax
from jax.sharding import PartitionSpec as P

HEAD_SIZE = 128


def merge_slices(numerator, factor_sum, maxima, totals):
    peak_all = jnp.max(maxima, axis=-1)
    weight = jnp.exp(maxima - peak_all[..., None])
    numerator = jnp.sum(numerator * weight[..., None], axis=-2)
    factor_sum = jnp.sum(factor_sum * weight[..., None], axis=-2)
    totals = jnp.sum(totals * weight, axis=-1)
    return (numerator, factor_sum, peak_all, totals)


def attend_local(
    query_matrix,
    down_factors,
    paged_base_keys,
    paged_base_values,
    paged_down_factors,
    heads_kv,
    low_rank_width,
):
    item_count = query_matrix.shape[0]
    head_size = paged_base_keys.shape[-1] // heads_kv
    all_heads = query_matrix.shape[1] // head_size
    query_group_size = all_heads // heads_kv
    local_tokens = paged_base_keys.shape[0] * paged_base_keys.shape[1]
    score_scaling = head_size ** (-0.5)
    key_heads = paged_base_keys.reshape(local_tokens, heads_kv, head_size).transpose(1, 0, 2)
    value_heads = paged_base_values.reshape(local_tokens, heads_kv, head_size).transpose(1, 0, 2)
    factor_flat = paged_down_factors.reshape(local_tokens, 2 * low_rank_width)
    cached_key = factor_flat[:, :low_rank_width]
    cached_value = factor_flat[:, low_rank_width:]
    query_head_count = query_matrix.reshape(
        item_count, heads_kv, query_group_size, head_size
    ).transpose(1, 0, 2, 3)
    factor_heads = down_factors.reshape(
        item_count, heads_kv, query_group_size, low_rank_width
    ).transpose(1, 0, 2, 3)

    def one_head(bundle):
        query_one, factor_one, key_one, value_one = bundle
        scores = (
            jnp.einsum("ngd,ld->ngl", query_one, key_one, preferred_element_type=jnp.float32)
            + jnp.einsum("ngj,lj->ngl", factor_one, cached_key, preferred_element_type=jnp.float32)
        ) * score_scaling
        maxima = jnp.max(scores, -1)
        weights = jnp.exp(scores - maxima[..., None])
        totals = jnp.sum(weights, -1)
        rounded = weights.astype(jnp.bfloat16)
        numerator = jnp.einsum(
            "ngl,ld->ngd", rounded, value_one, preferred_element_type=jnp.float32
        )
        factor_sum = jnp.einsum(
            "ngl,lj->ngj", rounded, cached_value, preferred_element_type=jnp.float32
        )
        return (numerator, factor_sum, maxima, totals)

    numerator, factor_sum, maxima, totals = lax.map(
        one_head, (query_head_count, factor_heads, key_heads, value_heads)
    )
    numerator = numerator.transpose(1, 0, 2, 3).reshape(item_count, all_heads, head_size)
    factor_sum = factor_sum.transpose(1, 0, 2, 3).reshape(item_count, all_heads, low_rank_width)
    maxima = maxima.transpose(1, 0, 2).reshape(item_count, all_heads)
    totals = totals.transpose(1, 0, 2).reshape(item_count, all_heads)
    return (numerator, factor_sum, maxima, totals)


def per_device(
    residual_input,
    input_norm_gain,
    query_weight,
    key_value_weight,
    shared_down_factors,
    query_up_factors,
    key_value_up_factors,
    paged_base_keys,
    paged_base_values,
    paged_down_factors,
    adapter_of_row,
    document_of_row,
    document_page_slots,
):
    tp_count = lax.axis_size("tp")
    grp_count = lax.axis_size("grp")
    tp_index = lax.axis_index("tp")
    low_rank_width = shared_down_factors.shape[1] // 3
    key_value_width = key_value_up_factors.shape[2] // 2
    head_size = HEAD_SIZE
    heads_kv = key_value_width // head_size
    row_count = residual_input.shape[0]
    score_scaling = head_size ** (-0.5)
    gathered = lax.all_gather(residual_input, "tp", axis=1, tiled=True).astype(jnp.float32)
    normed_input = (
        gathered
        * lax.rsqrt(jnp.mean(gathered * gathered, -1, keepdims=True) + 1e-06)
        * input_norm_gain
    ).astype(jnp.bfloat16)
    low_rank_part = jnp.dot(
        normed_input, shared_down_factors, preferred_element_type=jnp.float32
    ).astype(jnp.bfloat16)
    query_low_rank = low_rank_part[:, :low_rank_width]
    key_low_rank = low_rank_part[:, low_rank_width : 2 * low_rank_width]
    value_low_rank = low_rank_part[:, 2 * low_rank_width :]
    query_update = query_up_factors[adapter_of_row]
    query_part = (
        jnp.dot(normed_input, query_weight, preferred_element_type=jnp.float32)
        + jnp.einsum("ep,epg->eg", query_low_rank, query_update, preferred_element_type=jnp.float32)
    ).astype(jnp.bfloat16)
    key_value_columns = key_value_weight.shape[1]
    key_value_start = tp_index * key_value_columns
    key_value_update = lax.dynamic_slice_in_dim(
        key_value_up_factors, key_value_start, key_value_columns, 2
    )[adapter_of_row]
    key_value_low = jnp.where(key_value_start < key_value_width, key_low_rank, value_low_rank)
    kv_part = (
        jnp.dot(normed_input, key_value_weight, preferred_element_type=jnp.float32)
        + jnp.einsum(
            "ep,epg->eg", key_value_low, key_value_update, preferred_element_type=jnp.float32
        )
    ).astype(jnp.bfloat16)
    heads_here = query_part.shape[1] // head_size
    query_group_size = heads_here * tp_count // heads_kv
    key_value_head = tp_index * heads_here // query_group_size
    key_column_count = lax.dynamic_slice_in_dim(
        key_value_up_factors, key_value_head * head_size, head_size, 2
    )[adapter_of_row]
    my_queries = query_part.reshape(row_count, heads_here, head_size)
    factor_part = jnp.einsum(
        "rhd,rjd->rhj", my_queries, key_column_count, preferred_element_type=jnp.float32
    ).astype(jnp.bfloat16)
    factor_part = factor_part.reshape(row_count, heads_here * low_rank_width)
    query_matrix, down_factors, fresh_kv = (
        lax.all_gather(query_part, "tp", axis=1, tiled=True),
        lax.all_gather(factor_part, "tp", axis=1, tiled=True),
        lax.all_gather(kv_part, "tp", axis=1, tiled=True),
    )
    doc_pages = document_page_slots.shape[1]
    owner_of_doc = document_page_slots[:, 0] // doc_pages
    doc_ids = document_of_row[:, 0]
    doc_match = (doc_ids[:, None] == jnp.arange(document_page_slots.shape[0])[None, :]).astype(
        jnp.int32
    )
    target = jnp.sum(doc_match * owner_of_doc[None, :], 1)
    target_match = (target[:, None] == jnp.arange(grp_count)[None, :]).astype(jnp.int32)
    earlier = jnp.cumsum(target_match, 0) - target_match
    capacity = 2 * row_count // grp_count
    slot_of = target * capacity + jnp.sum(earlier * target_match, 1)
    placing = (jnp.arange(grp_count * capacity)[:, None] == slot_of[None, :]).astype(jnp.bfloat16)
    send_queries = (
        jnp.dot(placing, query_matrix, preferred_element_type=jnp.float32)
        .astype(jnp.bfloat16)
        .reshape(grp_count, capacity, -1)
    )
    send_factors = (
        jnp.dot(placing, down_factors, preferred_element_type=jnp.float32)
        .astype(jnp.bfloat16)
        .reshape(grp_count, capacity, -1)
    )
    query_in = lax.all_to_all(send_queries, "grp", split_axis=0, concat_axis=0, tiled=True)
    factor_in = lax.all_to_all(send_factors, "grp", split_axis=0, concat_axis=0, tiled=True)
    per_source = query_in.shape[1]
    item_count = query_in.shape[0] * per_source
    query_flat = query_in.reshape(item_count, -1)
    factor_flat = factor_in.reshape(item_count, -1)
    numerator, factor_sum, maxima, totals = attend_local(
        query_flat,
        factor_flat,
        paged_base_keys,
        paged_base_values,
        paged_down_factors,
        heads_kv,
        low_rank_width,
    )
    all_heads = numerator.shape[1]
    returned = (
        lax.all_to_all(
            numerator.reshape(grp_count, per_source, all_heads, head_size),
            "grp",
            split_axis=0,
            concat_axis=0,
            tiled=True,
        ),
        lax.all_to_all(
            factor_sum.reshape(grp_count, per_source, all_heads, low_rank_width),
            "grp",
            split_axis=0,
            concat_axis=0,
            tiled=True,
        ),
        lax.all_to_all(
            maxima.reshape(grp_count, per_source, all_heads),
            "grp",
            split_axis=0,
            concat_axis=0,
            tiled=True,
        ),
        lax.all_to_all(
            totals.reshape(grp_count, per_source, all_heads),
            "grp",
            split_axis=0,
            concat_axis=0,
            tiled=True,
        ),
    )
    numerator, factor_sum, maxima, totals = [
        piece.reshape((grp_count * capacity,) + piece.shape[2:])[slot_of] for piece in returned
    ]
    numerator, factor_sum, maxima, totals = (
        lax.all_to_all(numerator[:, :, None, :], "tp", split_axis=1, concat_axis=2, tiled=True),
        lax.all_to_all(factor_sum[:, :, None, :], "tp", split_axis=1, concat_axis=2, tiled=True),
        lax.all_to_all(maxima[:, :, None], "tp", split_axis=1, concat_axis=2, tiled=True),
        lax.all_to_all(totals[:, :, None], "tp", split_axis=1, concat_axis=2, tiled=True),
    )
    numerator, factor_sum, maxima, totals = merge_slices(numerator, factor_sum, maxima, totals)
    own_key = lax.dynamic_slice_in_dim(fresh_kv, key_value_head * head_size, head_size, 1)
    value_own = lax.dynamic_slice_in_dim(
        fresh_kv, key_value_width + key_value_head * head_size, head_size, 1
    )
    own_token_score = (
        jnp.einsum("rhd,rd->rh", my_queries, own_key, preferred_element_type=jnp.float32)
        * score_scaling
    )
    peak_all = jnp.maximum(maxima, own_token_score)
    old_scale = jnp.exp(maxima - peak_all)
    own_weight = jnp.exp(own_token_score - peak_all)
    numerator = (
        numerator * old_scale[..., None]
        + own_weight[..., None] * value_own.astype(jnp.float32)[:, None, :]
    )
    factor_sum = factor_sum * old_scale[..., None]
    totals = totals * old_scale + own_weight
    value_column_count = lax.dynamic_slice_in_dim(
        key_value_up_factors, key_value_width + key_value_head * head_size, head_size, 2
    )[adapter_of_row]
    value_shift = jnp.einsum(
        "rhj,rjd->rhd",
        factor_sum,
        value_column_count.astype(jnp.float32),
        precision=lax.Precision.HIGHEST,
    )
    result = ((numerator + value_shift) / totals[..., None]).astype(jnp.bfloat16)
    return result.reshape(row_count, heads_here * head_size)


def solution(mesh):
    in_specs = (
        P("grp", "tp"),
        P(),
        P(None, "tp"),
        P(None, "tp"),
        P(),
        P(None, None, "tp"),
        P(),
        P(("grp", "tp"), None, None),
        P(("grp", "tp"), None, None),
        P(("grp", "tp"), None, None),
        P("grp"),
        P("grp", None),
        P(),
    )
    out_specs = P("grp", "tp")
    return jax.shard_map(
        per_device, mesh=mesh, in_specs=in_specs, out_specs=out_specs, check_vma=False
    )
```

profile of v0, /device:TPU:9, one launch (start us, length us, event | category | flops | bytes accessed | tf_op | source)
XLA Modules:
  0.0 365.8 jit_solution(5221450590914724505)
XLA Ops:
  8.1 2.5 gather_fusion
  10.6 38.6 %all-gather.3.cloned.1.call-done = bf16[128,5120]{0,1:T(8,128)(2,1)} async-done(((bf16[128,320]{0,1:T(8,128)(2,1)}), bf16[128,5120]{0,1:T(8,128)(2,1)}) %all-gather.3.cloned.1.call-update) | async-done | bytes 1310736 | tf_op jit(solution)/shard_map/all_gather | solution.py:97
  49.1 2.0 fusion.18
  51.2 3.5 convolution_convert_fusion.3
  55.5 1.5 fusion.40
  57.0 3.2 fusion.22
  64.0 18.0 %all_gather.14 = bf16[128,512]{0,1:T(8,128)(2,1)S(1)} all-gather(bf16[128,32]{0,1:T(8,128)(2,1)S(1)} %bitcast.163), channel_id=1, replica_groups=mesh['grp'=2,'tp'=16] {'tp'}, dimensions={1}, use_global_device_ids=true | all-gather | bytes 139264 | tf_op jit(solution)/shard_map/all_gather | solution.py:139
  83.0 3.4 all-to-all-start.1
  86.4 10.6 %all-gather.5.cloned.1.call-done = bf16[128,4096]{1,0:T(8,128)(2,1)} async-done(((bf16[128,256]{1,0:T(8,128)(2,1)}), bf16[128,4096]{1,0:T(8,128)(2,1)}) %all-gather.5.cloned.1.call-update) | async-done | bytes 1048592 | tf_op jit(solution)/shard_map/all_gather | solution.py:138
  97.0 3.2 convolution_convert_fusion
  100.3 5.0 %all-to-all-start = ((bf16[2,128,4096]{2,1,0:T(8,128)(2,1)}), bf16[2,128,4096]{2,1,0:T(8,128)(2,1)}, u32[]{:S(2)}, u32[]{:S(2)}) async-start(bf16[2,128,4096]{2,1,0:T(8,128)(2,1)} %bitcast.146), calls=%async_computation | async-start | bytes 4194304 | tf_op jit(solution)/shard_map/all_to_all | solution.py:164
  105.3 1.0 reshape.113
  106.3 1.1 copy.100
  107.4 2.0 reshape.118
  109.4 2.0 copy.101
  112.2 1.1 reshape_reshape.19
  113.3 16.7 %all-to-all-done = bf16[2,128,4096]{2,1,0:T(8,128)(2,1)} async-done(((bf16[2,128,4096]{2,1,0:T(8,128)(2,1)}), bf16[2,128,4096]{2,1,0:T(8,128)(2,1)}, u32[]{:S(2)}, u32[]{:S(2)}) %all-to-all-start) | async-done | bytes 2097184 | tf_op jit(solution)/shard_map/all_to_all | solution.py:164
  130.1 3.4 copy.134
  133.5 34.6 %while.16 = (s32[]{:T(128)}, f32[4,256,8,128]{3,1,2,0:T(8,128)}, f32[4,256,8,16]{1,3,2,0:T(8,128)}, f32[4,256,8]{1,2,0:T(8,128)}, f32[4,256,8]{1,2,0:T(8,128)S(1...) while((s32[]{:T(128)}, f32[4,256,8,128]{3,1,2,0:T(8,128)}, ...), condition=%wide.region_7.8_spmd, body=%wide.region_4.7_spmd.sunk | while | flops 613412864 | bytes 28353680 | solution.py:63
  133.5 1.1 constant_dynamic-slice_fusion.5
  136.1 1.2 fusion.72
  137.9 1.5 fusion.71
  139.4 2.7 fusion.70
  142.1 1.1 constant_dynamic-slice_fusion.5
  144.7 1.2 fusion.72
  146.5 1.5 fusion.71
  148.0 2.7 fusion.70
  150.8 1.1 constant_dynamic-slice_fusion.5
  153.4 1.2 fusion.72
  155.2 1.5 fusion.71
  156.7 2.7 fusion.70
  159.4 1.1 constant_dynamic-slice_fusion.5
  162.0 1.2 fusion.72
  163.8 1.5 fusion.71
  165.3 2.7 fusion.70
  169.4 3.3 all-to-all-start.4
  173.4 2.1 all-to-all-done.4
  175.5 3.3 all-to-all-start.8
  180.2 1.3 all-to-all-done.8
  181.5 7.6 %all-to-all-start.5 = ((f32[128,32,1]{0,2,1:T(1,128)}), f32[128,32,1]{0,2,1:T(1,128)S(1)}, u32[]{:S(2)}, u32[]{:S(2)}) async-start(f32[128,32,1]{0,2,1:T(1,128)} %copy.106), calls=%async_computation.5 | async-start | bytes 32768 | tf_op jit(solution)/shard_map/all_to_all | solution.py:216
  190.6 3.6 all-to-all-done.5
  194.2 4.9 %all-to-all-start.9 = ((f32[128,32,1]{0,2,1:T(1,128)}), f32[128,32,1]{0,2,1:T(1,128)S(1)}, u32[]{:S(2)}, u32[]{:S(2)}) async-start(f32[128,32,1]{0,2,1:T(1,128)} %copy.117), calls=%async_computation.9 | async-start | bytes 32768 | tf_op jit(solution)/shard_map/all_to_all | solution.py:217
  199.0 1.3 reshape_reshape.22
  201.2 2.9 all-to-all-done.9
  204.1 3.7 %all-to-all-start.6 = ((f32[2,128,32,16]{1,3,2,0:T(8,128)}), f32[2,128,32,16]{1,3,2,0:T(8,128)S(1)}, u32[]{:S(2)}, u32[]{:S(2)}) async-start(f32[2,128,32,16]{1,3,2,0:T(8,128)} %copy.111), calls=%async_computation.6 | async-start | bytes 1048576 | tf_op jit(solution)/shard_map/all_to_all | solution.py:188
  207.7 6.6 %copy.102 = f32[2,128,32,128]{3,2,1,0:T(8,128)} copy(f32[2,128,32,128]{3,1,0,2:T(8,128)} %bitcast.148) | data formatting | bytes 8388608 | tf_op jit(solution)/shard_map/reshape;reshape | solution.py:182
  214.3 1.1 all-to-all-done.6
  215.4 5.6 %all-to-all-start.2 = ((f32[2,128,32,128]{3,2,1,0:T(8,128)}), f32[2,128,32,128]{3,2,1,0:T(8,128)}, u32[]{:S(2)}, u32[]{:S(2)}) async-start(f32[2,128,32,128]{3,2,1,0:T(8,128)} %copy.102), calls=%async_computation.2 | async-start | bytes 8388608 | tf_op jit(solution)/shard_map/all_to_all | solution.py:181
  221.0 2.2 copy.112
  223.2 3.2 gather_fusion.5
  226.4 2.4 copy.113
  228.9 38.4 %all-to-all-done.2 = f32[2,128,32,128]{3,2,1,0:T(8,128)} async-done(((f32[2,128,32,128]{3,2,1,0:T(8,128)}), f32[2,128,32,128]{3,2,1,0:T(8,128)}, u32[]{:S(2)}, u32[]{:S(2)}) %all-to-all-start.2) | async-done | bytes 4194336 | tf_op jit(solution)/shard_map/all_to_all | solution.py:181
  267.2 5.9 %all-to-all-start.7 = ((f32[128,32,1,16]{0,3,2,1:T(8,128)}), f32[128,32,1,16]{0,3,2,1:T(8,128)S(1)}, u32[]{:S(2)}, u32[]{:S(2)}) async-start(f32[128,32,1,16]{0,3,2,1:T(8,128)} %copy.113), calls=%async_computation.7 | async-start | bytes 524288 | tf_op jit(solution)/shard_map/all_to_all | solution.py:215
  273.1 4.2 %gather_fusion.2 = f32[128,32,128]{2,1,0:T(8,128)} fusion(f32[256,32,128]{2,1,0:T(8,128)} %bitcast.25, s32[1024]{0:T(1024)S(1)} %pad_clamp_fusion), kind=kCustom, calls=%fused_computation.2 | custom fusion | bytes 4194816 | tf_op jit(solution)/shard_map/gather | solution.py:211
  277.3 4.1 %copy.103 = f32[128,32,1,128]{3,0,2,1:T(8,128)} copy(f32[128,32,1,128]{3,1,0,2:T(8,128)} %bitcast.147) | data formatting | bytes 4194304 | tf_op jit(solution)/shard_map/broadcast_in_dim | solution.py:214
  281.9 5.7 %all-to-all-start.3 = ((f32[128,32,1,128]{3,0,2,1:T(8,128)}), f32[128,32,1,128]{3,0,2,1:T(8,128)}, u32[]{:S(2)}, u32[]{:S(2)}) async-start(f32[128,32,1,128]{3,0,2,1:T(8,128)} %copy.103), calls=%async_computation.3 | async-start | bytes 4194304 | tf_op jit(solution)/shard_map/all_to_all | solution.py:214
  287.6 1.6 gather_fusion.6
  291.9 1.0 multiply_reduce_fusion.1
  293.8 2.5 fusion.24
  296.3 49.9 %all_gather.15 = bf16[128,1024]{0,1:T(8,128)(2,1)S(1)} all-gather(bf16[128,64]{0,1:T(8,128)(2,1)S(1)} %fusion.24), channel_id=1, replica_groups=mesh['grp'=2,'tp'=16] {'tp'}, dimensions={1}, use_global_device_ids=true | all-gather | bytes 278528 | tf_op jit(solution)/shard_map/all_gather | solution.py:140
  346.9 1.6 copy.110
  349.2 1.1 multiply_reduce_fusion.3
  354.8 1.9 multiply_reduce_fusion
  356.7 1.6 fusion.23
  (102 shorter events, 32.7 us)
Async XLA Ops:
  6.5 50.5 %copy-start = (bf16[5120,256]{1,0:T(8,128)(2,1)S(1)}, bf16[5120,256]{1,0:T(8,128)(2,1)}, u32[]{:S(2)}) copy-start(bf16[5120,256]{1,0:T(8,128)(2,1)} %param.17) | copy-start | bytes 7864324
  6.5 44.6 %copy-start.10 = (f32[5120]{0:T(1024)S(1)}, f32[5120]{0:T(1024)}, u32[]{:S(2)}) copy-start(f32[5120]{0:T(1024)} %param.16) | copy-start | bytes 61444
  6.5 44.6 %copy-start.9 = (bf16[5120,48]{0,1:T(8,128)(2,1)S(1)}, bf16[5120,48]{0,1:T(8,128)(2,1)}, u32[]{:S(2)}) copy-start(bf16[5120,48]{0,1:T(8,128)(2,1)} %param.19) | copy-start | bytes 1474564
  6.5 42.6 %all-gather.3.cloned.1.call-start = ((), (), s32[]{:S(2)}) async-start(), calls=%async_computation.10 | async-start | bytes 1392640 | tf_op jit(solution)/shard_map/all_gather | solution.py:97
  7.3 89.8 %all-gather.5.cloned.1.call-start = ((), (), s32[]{:S(2)}) async-start(), calls=%async_computation.11 | async-start | bytes 1114112 | tf_op jit(solution)/shard_map/all_gather | solution.py:138
  8.1 53.7 %copy-start.8 = (s32[1024]{0:T(1024)}, s32[1024]{0:T(1024)S(1)}, u32[]{:S(2)}) copy-start(s32[1024]{0:T(1024)S(1)} %pad_clamp_fusion.1) | copy-start | bytes 12292
  51.2 9.0 %copy-start.13 = (f32[128]{0:T(128)}, f32[128]{0:T(128)S(1)}, u32[]{:S(2)}) copy-start(f32[128]{0:T(128)S(1)} %add_rsqrt_fusion) | copy-start | bytes 1540
  55.4 4.8 %copy-start.11 = (s32[2,64]{1,0:T(2,128)S(1)}, s32[2,64]{1,0:T(2,128)}, u32[]{:S(2)}) copy-start(s32[2,64]{1,0:T(2,128)} %param.27) | copy-start | bytes 1540
  55.5 4.9 %copy-start.12 = (s32[128,1]{0,1:T(1,128)S(1)}, s32[128,1]{0,1:T(1,128)}, u32[]{:S(2)}) copy-start(s32[128,1]{0,1:T(1,128)} %param.26) | copy-start | bytes 1540
  63.5 33.5 %copy-start.3 = (bf16[128,2,128]{2,1,0:T(2,128)(2,1)}, bf16[128,2,128]{2,1,0:T(2,128)(2,1)S(1)}, u32[]{:S(2)}) copy-start(bf16[128,2,128]{2,1,0:T(2,128)(2,1)S(1)} %reshape.114) | copy-start | bytes 196612
  83.0 17.3 %all-to-all-start.1 = ((bf16[2,128,512]{2,1,0:T(8,128)(2,1)}), bf16[2,128,512]{2,1,0:T(8,128)(2,1)S(1)}, u32[]{:S(2)}, u32[]{:S(2)}) async-start(bf16[2,128,512]{2,1,0:T(8,128)(2,1)} %bitcast.20), calls=%async_computation.1 | async-start | bytes 524288 | tf_op jit(solution)/shard_map/all_to_all | solution.py:165
  100.3 5.0 %copy-start.1 = (bf16[4,128,512]{2,1,0:T(8,128)(2,1)S(1)}, bf16[4,128,512]{2,1,0:T(8,128)(2,1)}, u32[]{:S(2)}) copy-start(bf16[4,128,512]{2,1,0:T(8,128)(2,1)} %param.22) | copy-start | bytes 1572868
  100.3 29.8 %all-to-all-start = ((bf16[2,128,4096]{2,1,0:T(8,128)(2,1)}), bf16[2,128,4096]{2,1,0:T(8,128)(2,1)}, u32[]{:S(2)}, u32[]{:S(2)}) async-start(bf16[2,128,4096]{2,1,0:T(8,128)(2,1)} %bitcast.146), calls=%async_computation | async-start | bytes 4194304 | tf_op jit(solution)/shard_map/all_to_all | solution.py:164
  105.3 6.1 %copy-start.7 = (bf16[4,128,32]{1,2,0:T(8,128)(2,1)S(1)}, bf16[4,128,32]{1,2,0:T(8,128)(2,1)}, u32[]{:S(2)}) copy-start(bf16[4,128,32]{1,2,0:T(8,128)(2,1)} %param.24) | copy-start | bytes 98308
  169.4 6.0 %all-to-all-start.4 = ((f32[2,128,32]{1,2,0:T(8,128)}), f32[2,128,32]{1,2,0:T(8,128)S(1)}, u32[]{:S(2)}, u32[]{:S(2)}) async-start(f32[2,128,32]{1,2,0:T(8,128)} %copy.104), calls=%async_computation.4 | async-start | bytes 65536 | tf_op jit(solution)/shard_map/all_to_all | solution.py:195
  175.5 6.0 %all-to-all-start.8 = ((f32[2,128,32]{1,2,0:T(8,128)}), f32[2,128,32]{1,2,0:T(8,128)S(1)}, u32[]{:S(2)}, u32[]{:S(2)}) async-start(f32[2,128,32]{1,2,0:T(8,128)} %copy.115), calls=%async_computation.8 | async-start | bytes 65536 | tf_op jit(solution)/shard_map/all_to_all | solution.py:202
  181.5 12.6 %all-to-all-start.5 = ((f32[128,32,1]{0,2,1:T(1,128)}), f32[128,32,1]{0,2,1:T(1,128)S(1)}, u32[]{:S(2)}, u32[]{:S(2)}) async-start(f32[128,32,1]{0,2,1:T(1,128)} %copy.106), calls=%async_computation.5 | async-start | bytes 32768 | tf_op jit(solution)/shard_map/all_to_all | solution.py:216
  194.2 9.9 %all-to-all-start.9 = ((f32[128,32,1]{0,2,1:T(1,128)}), f32[128,32,1]{0,2,1:T(1,128)S(1)}, u32[]{:S(2)}, u32[]{:S(2)}) async-start(f32[128,32,1]{0,2,1:T(1,128)} %copy.117), calls=%async_computation.9 | async-start | bytes 32768 | tf_op jit(solution)/shard_map/all_to_all | solution.py:217
  204.1 10.3 %copy-start.6 = (f32[128,32,1]{0,2,1:T(1,128)}, f32[128,32,1]{0,2,1:T(1,128)S(1)}, u32[]{:S(2)}) copy-start(f32[128,32,1]{0,2,1:T(1,128)S(1)} %all-to-all-done.9) | copy-start | bytes 49156
  204.1 11.4 %all-to-all-start.6 = ((f32[2,128,32,16]{1,3,2,0:T(8,128)}), f32[2,128,32,16]{1,3,2,0:T(8,128)S(1)}, u32[]{:S(2)}, u32[]{:S(2)}) async-start(f32[2,128,32,16]{1,3,2,0:T(8,128)} %copy.111), calls=%async_computation.6 | async-start | bytes 1048576 | tf_op jit(solution)/shard_map/all_to_all | solution.py:188
  215.4 51.8 %all-to-all-start.2 = ((f32[2,128,32,128]{3,2,1,0:T(8,128)}), f32[2,128,32,128]{3,2,1,0:T(8,128)}, u32[]{:S(2)}, u32[]{:S(2)}) async-start(f32[2,128,32,128]{3,2,1,0:T(8,128)} %copy.102), calls=%async_computation.2 | async-start | bytes 8388608 | tf_op jit(solution)/shard_map/all_to_all | solution.py:181
  267.2 14.6 %all-to-all-start.7 = ((f32[128,32,1,16]{0,3,2,1:T(8,128)}), f32[128,32,1,16]{0,3,2,1:T(8,128)S(1)}, u32[]{:S(2)}, u32[]{:S(2)}) async-start(f32[128,32,1,16]{0,3,2,1:T(8,128)} %copy.113), calls=%async_computation.7 | async-start | bytes 524288 | tf_op jit(solution)/shard_map/all_to_all | solution.py:215
  281.9 72.9 %all-to-all-start.3 = ((f32[128,32,1,128]{3,0,2,1:T(8,128)}), f32[128,32,1,128]{3,0,2,1:T(8,128)}, u32[]{:S(2)}, u32[]{:S(2)}) async-start(f32[128,32,1,128]{3,0,2,1:T(8,128)} %copy.103), calls=%async_computation.3 | async-start | bytes 4194304 | tf_op jit(solution)/shard_map/all_to_all | solution.py:214
  290.1 59.1 %copy-start.4 = (bf16[128,2,128]{2,1,0:T(2,128)(2,1)S(1)}, bf16[128,2,128]{2,1,0:T(2,128)(2,1)}, u32[]{:S(2)}) copy-start(bf16[128,2,128]{2,1,0:T(2,128)(2,1)} %copy-done.3) | copy-start | bytes 196612
  296.3 60.4 %copy-start.2 = (bf16[128,16,128]{2,1,0:T(8,128)(2,1)S(1)}, bf16[128,16,128]{2,1,0:T(8,128)(2,1)}, u32[]{:S(2)}) copy-start(bf16[128,16,128]{2,1,0:T(8,128)(2,1)} %gather_fusion.6) | copy-start | bytes 1572868
  350.2 6.5 %copy-start.5 = (f32[128,128]{1,0:T(8,128)S(1)}, f32[128,128]{1,0:T(8,128)}, u32[]{:S(2)}) copy-start(f32[128,128]{1,0:T(8,128)} %copy.110) | copy-start | bytes 196612
Sparse Core Ops, SparseCore 0:
  9.6 39.4 all-gather.2
  60.4 36.6 all-gather.4
where the time goes:
time: 368 us; the launch traced here: 366 us
  waiting for transfers between devices  116 us (32%)
  blocking collectives  68 us (18%)
  local copies, waits for them, and re-layouts  64.4 us (18%)
  starting transfers between devices  48.3 us (13%)
  matrix products  40 us (11%)
  other arithmetic  14.9 us (4%)
  between operations  13.8 us (4%)
    all_gather x1, blocking collectives, per_device(): lax.all_gather(kv_part, 'tp', axis=1, tiled=True)  49.9 us
    all_gather x1, waiting for transfers between devices, per_device(): lax.all_gather(residual_input, 'tp', axis=1, tiled=True).astype(jnp.float32)  38.6 us
    all_to_all x1, waiting for transfers between devices, per_device(): lax.all_to_all(numerator.reshape(grp_count, per_source, all_heads, head_s...  38.4 us
    all_gather x1, blocking collectives, per_device(): lax.all_gather(factor_part, 'tp', axis=1, tiled=True)  18 us
    all_to_all x1, waiting for transfers between devices, per_device(): lax.all_to_all(send_queries, 'grp', split_axis=0, concat_axis=0, tiled=True)  16.7 us
    dot_general x4, matrix products, one_head(): jnp.einsum('ngl,ld->ngd', rounded, value_one, preferred_element_type=jnp....  10.8 us
    all_gather x1, waiting for transfers between devices, per_device(): lax.all_gather(query_part, 'tp', axis=1, tiled=True)  10.6 us
    gather x4, local copies, waits for them, and re-layouts, per_device(): piece.reshape((grp_count * capacity,) + piece.shape[2:])[slot_of]  8.72 us
  transfers between devices with their start and end apart: 12, of which 10 were waited for; matrix products, arithmetic and copies ran while one was open for 18% of the time, Pallas kernels for 0%

commit v1 on v0

--- a/solution.py
+++ b/solution.py
@@ -1,9 +1,440 @@
+import functools
+import math
+
 import jax
 import jax.numpy as jnp
 from jax import lax
+from jax.experimental import pallas as pl
+from jax.experimental.pallas import tpu as pltpu
 from jax.sharding import PartitionSpec as P
 
 HEAD_SIZE = 128
+MESH = pl.DeviceIdType.MESH
+F32 = jnp.float32
+BF16 = jnp.bfloat16
+
+
+def dot(a, b):
+    return jnp.dot(a, b, preferred_element_type=F32)
+
+
+def dot_nt(a, b):
+    return lax.dot_general(a, b, (((1,), (1,)), ((), ())), preferred_element_type=F32)
+
+
+def lanes(shape):
+    return lax.broadcasted_iota(jnp.int32, shape, len(shape) - 1)
+
+
+def split_three(value):
+    high = value.astype(BF16).astype(F32)
+    middle = (value - high).astype(BF16).astype(F32)
+    low = (value - high - middle).astype(BF16).astype(F32)
+    return high, middle, low
+
+
+def fused_kernel(
+    x_ref, gain_ref, qw_hbm, kvw_hbm, dn_hbm, qu_ref, ku_ref, k_hbm, v_hbm, d_ref,
+    adapter_ref, doc_ref, slots_ref, out_ref,
+    xbuf, qw, kvw, dn, wo, yq, yo, ssq, kbuf, vbuf, dbuf, qbuf, lhs, kaug, vaug,
+    acc, peak, psend, pbuf, fresh, fresh_in,
+    load_sem, x_send, x_recv, kv_send, kv_recv, q_send, q_recv, f_send, f_recv, p_send, p_recv,
+):
+    rows = x_ref.shape[0]
+    chunk = x_ref.shape[1]
+    width = 16 * chunk
+    grp = lax.axis_index("grp")
+    tp = lax.axis_index("tp")
+    z = tp // 4
+    s = tp % 4
+    y = s // 2
+    c = s % 2
+    scale = math.log2(math.e) / math.sqrt(HEAD_SIZE)
+
+    def at(g, t):
+        return {"grp": g, "tp": t}
+
+    sibling = at(grp, z * 4 + y * 2 + (1 - c))
+    across = at(grp, z * 4 + (1 - y) * 2 + c)
+    z_others = [z + 1 - 2 * (z % 2), (z + 2) % 4, 3 - z]
+
+    loads = [
+        pltpu.make_async_copy(src, dst, load_sem.at[i])
+        for i, (src, dst) in enumerate(
+            ((kvw_hbm, kvw), (dn_hbm, dn), (qw_hbm, qw),
+             (k_hbm.at[:, :, pl.ds(pl.multiple_of(z * 128, 128), 128)], kbuf.at[z]),
+             (v_hbm.at[:, :, pl.ds(pl.multiple_of(z * 128, 128), 128)], vbuf.at[z]))
+        )
+    ]
+    for load in loads:
+        load.start()
+
+    barrier = pltpu.get_barrier_semaphore()
+    for i in range(1, 16):
+        pl.semaphore_signal(barrier, inc=1, device_id=at(grp, (tp + i) % 16), device_id_type=MESH)
+    for j in range(4):
+        pl.semaphore_signal(barrier, inc=1, device_id=at(1 - grp, z * 4 + j), device_id_type=MESH)
+    xbuf[tp] = x_ref[...]
+    dbuf[z] = jnp.concatenate([d_ref[p] for p in range(4)], axis=1)
+    pl.semaphore_wait(barrier, 19)
+
+    started = []
+
+    def send(src, dst, send_sem, recv_sem, device):
+        copy = pltpu.make_async_remote_copy(
+            src_ref=src, dst_ref=dst, send_sem=send_sem, recv_sem=recv_sem,
+            device_id=device, device_id_type=MESH,
+        )
+        copy.start()
+        return copy
+
+    def arrive(dst, send_sem, recv_sem):
+        pltpu.make_async_remote_copy(
+            src_ref=dst, dst_ref=dst, send_sem=send_sem, recv_sem=recv_sem,
+            device_id=sibling, device_id_type=MESH,
+        ).wait_recv()
+
+    def send_x(t, sem, device):
+        copy = send(xbuf.at[t], xbuf.at[t], x_send.at[sem], x_recv.at[t], device)
+        started.append(copy)
+        return copy
+
+    first = [send_x(tp, i, at(grp, zo * 4 + s)) for i, zo in enumerate(z_others)]
+    send_x(tp, 3, across)
+    send_x(tp, 7, sibling)
+
+    loads[0].wait()
+    loads[1].wait()
+
+    def join(i, carry):
+        part = pl.ds(pl.multiple_of(i * chunk, 64), chunk)
+        wo[part, :] = jnp.concatenate(
+            [kvw[part, :], dn[part, :], jnp.zeros((chunk, 16), BF16)], axis=1
+        )
+        return carry
+
+    lax.fori_loop(0, 16, join, 0)
+    yq[...] = jnp.zeros_like(yq)
+    yo[...] = jnp.zeros_like(yo)
+    ssq[...] = jnp.zeros_like(ssq)
+    loads[2].wait()
+
+    def project(t):
+        block = xbuf[t].astype(F32)
+        ssq[...] += jnp.sum(block * block, axis=-1, keepdims=True)
+        scaled = (block * gain_ref[pl.ds(t, 1), :]).astype(BF16)
+        part = pl.ds(pl.multiple_of(t * chunk, 64), chunk)
+        yq[...] += dot(scaled, qw[part, :])
+        yo[...] += dot(scaled, wo[part, :])
+
+    project(tp)
+    for copy in first:
+        copy.wait_send()
+        started.remove(copy)
+    for n, i in enumerate((1, 2, 0)):
+        zo = z_others[i]
+        cols = pl.ds(pl.multiple_of(zo * 128, 128), 128)
+        device = at(grp, zo * 4 + s)
+        for n2, (src, dst) in enumerate(
+            ((k_hbm.at[:, :, cols], kbuf), (v_hbm.at[:, :, cols], vbuf), (dbuf.at[z], dbuf))
+        ):
+            started.append(
+                send(src, dst.at[z], kv_send.at[i * 3 + n2], kv_recv.at[z * 3 + n2], device)
+            )
+    for i, zo in enumerate(z_others):
+        t = zo * 4 + s
+        arrive(xbuf.at[t], x_send.at[0], x_recv.at[t])
+        send_x(t, 4 + i, across)
+        send_x(t, 8 + i, sibling)
+        project(t)
+    for i, zo in enumerate([z] + z_others):
+        t = zo * 4 + (1 - y) * 2 + c
+        arrive(xbuf.at[t], x_send.at[0], x_recv.at[t])
+        send_x(t, 11 + i, sibling)
+        project(t)
+    for zo in [z] + z_others:
+        for yo_ in (y, 1 - y):
+            t = zo * 4 + yo_ * 2 + (1 - c)
+            arrive(xbuf.at[t], x_send.at[0], x_recv.at[t])
+            project(t)
+
+    rinv = lax.rsqrt(ssq[...] * (1.0 / width) + 1e-06)
+    other = yo[...] * rinv
+    low = other[:, 64:128].astype(BF16)
+    adapter = adapter_ref[...]
+    wide = lanes((rows, 256))
+    picked = (wide // 16) == adapter
+    row_of = lax.broadcasted_iota(jnp.int32, (64, 256), 0)
+    col_of = lanes((64, 256)) % 16
+
+    def spread(part, offset):
+        tile = (row_of == col_of + offset).astype(F32).astype(BF16)
+        return jnp.where(picked, dot(part, tile), 0.0).astype(BF16)
+
+    queries = (yq[...] * rinv + dot(spread(low, 0), qu_ref[...].reshape(256, 256))).astype(BF16)
+    odd = tp % 2
+    is_key = tp < 8
+    kv_low = jnp.where(is_key, spread(low, 16).astype(F32), spread(low, 32).astype(F32)).astype(BF16)
+    pair_cols = pl.ds(pl.multiple_of((tp // 2) * 128, 128), 128)
+    kv_update = dot(kv_low, ku_ref[:, :, pair_cols].reshape(256, 128))
+    kv_base = other[:, :64]
+    kv_full = jnp.concatenate([kv_base, kv_base], axis=1) + kv_update
+    narrow = lanes((rows, 128))
+    fresh[...] = jnp.where((narrow // 64) == odd, kv_full, 0.0).astype(BF16)
+    fold_row = lax.broadcasted_iota(jnp.int32, (256, 128), 0) % 16
+    fold_col = lanes((256, 128))
+    key_up = ku_ref[:, :, pl.ds(pl.multiple_of(z * 128, 128), 128)].reshape(256, 128)
+    factors = jnp.zeros((rows, 128), F32)
+    for h in range(2):
+        full = dot_nt(queries[:, h * 128 : (h + 1) * 128], key_up)
+        full = jnp.where(picked, full, 0.0).astype(BF16)
+        fold = (fold_col == fold_row + 16 * h).astype(F32).astype(BF16)
+        factors = factors + dot(full, fold)
+    mine = 4 * grp + s
+    qbuf[mine, :, :256] = queries
+    qbuf[mine, :, 256:] = factors.astype(BF16)
+
+    n = 0
+    for g, shift in ((1 - grp, 0), (1 - grp, 1), (1 - grp, 2), (1 - grp, 3), (grp, 1), (grp, 2), (grp, 3)):
+        device = at(g, z * 4 + (s + shift) % 4)
+        started.append(send(qbuf.at[mine], qbuf.at[mine], q_send.at[n], q_recv.at[mine], device))
+        n += 1
+    head = (tp % 8) // 2
+    slot = (tp // 8) * 2 + odd
+    for j in range(4):
+        target = head * 4 + j
+
+        @pl.when(target != tp)
+        def _():
+            send(fresh, fresh_in.at[slot], f_send.at[j], f_recv.at[slot], at(grp, target))
+
+        @pl.when(target == tp)
+        def _():
+            fresh_in[slot] = fresh[...]
+
+    def augment(zo):
+        for p in range(4):
+            part = pl.ds(p * 128, 128)
+            down = dbuf[zo, :, p * 32 : (p + 1) * 32]
+            kaug[part, :128] = kbuf[zo, p]
+            kaug[part, 128:] = jnp.concatenate(
+                [down[:, :16], down[:, :16], jnp.zeros((128, 96), BF16)], axis=1
+            )
+            right = jnp.concatenate([down[:, 16:], jnp.zeros((128, 112), BF16)], axis=1)
+            vaug[part, :128] = vbuf[zo, p]
+            vaug[part, 128:] = jnp.where(
+                lanes((128, 128)) == 16, 1.0, right.astype(F32)
+            ).astype(BF16)
+
+    def attend(j, start):
+        scores = dot_nt(lhs[j], kaug[...]) * scale
+        top = jnp.max(scores, axis=-1, keepdims=True)
+        if not start:
+            old = peak[j]
+            top = jnp.maximum(old, top)
+        weights = jnp.exp2(scores - top).astype(BF16)
+        product = dot(weights, vaug[...])
+        if start:
+            acc[j] = product
+        else:
+            acc[j] = acc[j] * jnp.exp2(old - top) + product
+        peak[j] = top
+
+    loads[3].wait()
+    loads[4].wait()
+    augment(z)
+    f_lane = lanes((rows, 128)) // 16
+    for shift in range(4):
+        j = (s + shift) % 4
+        for g, local in ((grp, True), (1 - grp, False)):
+            index = 4 * g + j
+            if not (local and shift == 0):
+                arrive(qbuf.at[index], x_send.at[0], q_recv.at[index])
+            extra = qbuf[index, :, 256:].astype(F32)
+            for h in range(2):
+                part = pl.ds(pl.multiple_of(h * 256 + g * 128, 128), 128)
+                lhs[j, part, :128] = qbuf[index, :, h * 128 : (h + 1) * 128]
+                lhs[j, part, 128:] = jnp.where(f_lane == h, extra, 0.0).astype(BF16)
+        attend(j, True)
+
+    def arrived(zo):
+        for n2, dst in enumerate((kbuf, vbuf, dbuf)):
+            arrive(dst.at[zo], x_send.at[0], kv_recv.at[zo * 3 + n2])
+
+    for zo in z_others[:2]:
+        arrived(zo)
+        augment(zo)
+
+        def body(j, carry):
+            attend(j, False)
+            return carry
+
+        lax.fori_loop(0, 4, body, 0)
+
+    arrived(z_others[2])
+    augment(z_others[2])
+
+    def last(shift, carry):
+        j = (s + shift) % 4
+        attend(j, False)
+        lane = lanes((128, 128))
+        for g in range(2):
+            stats = None
+            for h in range(2):
+                part = pl.ds(h * 256 + g * 128, 128)
+                psend[j, g, :, h * 128 : (h + 1) * 128] = acc[j, part, :128].astype(BF16)
+                tail = acc[j, part, 128:]
+                high = tail.astype(BF16).astype(F32)
+                m0, m1, m2 = split_three(peak[j, part, :])
+                one = high + pltpu.roll(tail - high, 32, 1)
+                one = jnp.where(lane == 24, m0, one)
+                one = jnp.where(lane == 25, m1, one)
+                one = jnp.where(lane == 26, m2, one)
+                stats = one if h == 0 else stats + pltpu.roll(one, 64, 1)
+            psend[j, g, :, 256:] = stats.astype(BF16)
+            here = jnp.logical_and(j == s, grp == g)
+
+            @pl.when(jnp.logical_not(here))
+            def _():
+                send(psend.at[j, g], pbuf.at[mine], p_send.at[j * 2 + g], p_recv.at[mine], at(g, z * 4 + j))
+
+            @pl.when(here)
+            def _():
+                pbuf[mine] = psend[j, g]
+
+        return carry
+
+    lax.fori_loop(1, 5, last, 0)
+
+    for n in range(4):
+        source = (n // 2) * 8 + 2 * z + n % 2
+
+        @pl.when(source != tp)
+        def _():
+            arrive(fresh_in.at[n], x_send.at[0], f_recv.at[n])
+
+    own_key = fresh_in[0].astype(F32) + fresh_in[1].astype(F32)
+    own_value = fresh_in[2].astype(F32) + fresh_in[3].astype(F32)
+    for n in range(1, 8):
+        index = (mine + n) % 8
+        arrive(pbuf.at[index], x_send.at[0], p_recv.at[index])
+    half = slots_ref.shape[1]
+    document = doc_ref[...]
+    holder = jnp.where(document == 0, slots_ref[0, 0] // half, slots_ref[1, 0] // half)
+    narrow = lanes((rows, 128))
+    picked = (lanes((rows, 256)) // 16) == adapter_ref[...]
+    value_up = ku_ref[:, :, pl.ds(pl.multiple_of(512 + z * 128, 128), 128)].reshape(256, 128)
+    row_of = lax.broadcasted_iota(jnp.int32, (128, 256), 0)
+    tile = (row_of == lanes((128, 256)) % 16).astype(F32).astype(BF16)
+    blocks = [
+        jnp.where(holder == 0, pbuf[j].astype(F32), pbuf[4 + j].astype(F32)) for j in range(4)
+    ]
+    for h in range(2):
+        query = qbuf[mine, :, h * 128 : (h + 1) * 128].astype(F32)
+        own = jnp.sum(query * own_key, axis=-1, keepdims=True) * scale
+        top = own
+        parts = []
+        for block in blocks:
+            stats = block[:, 256:]
+            if h:
+                stats = pltpu.roll(stats, 64, 1)
+            at_peak = jnp.logical_and(narrow >= 24, narrow < 27)
+            m = jnp.sum(jnp.where(at_peak, stats, 0.0), axis=-1, keepdims=True)
+            tail = jnp.where(narrow < 17, stats + pltpu.roll(stats, 96, 1), 0.0)
+            top = jnp.maximum(top, m)
+            parts.append((block[:, h * 128 : (h + 1) * 128], tail, m))
+        own_weight = jnp.exp2(own - top)
+        numerator = own_weight * own_value
+        tail_sum = jnp.zeros((rows, 128), F32)
+        for num, tail, m in parts:
+            weight = jnp.exp2(m - top)
+            numerator = numerator + num * weight
+            tail_sum = tail_sum + tail * weight
+        total = jnp.sum(jnp.where(narrow == 16, tail_sum, 0.0), axis=-1, keepdims=True) + own_weight
+        factor = jnp.where(narrow < 16, tail_sum, 0.0)
+        high = factor.astype(BF16)
+        shift = jnp.zeros((rows, 128), F32)
+        for piece in (high, (factor - high.astype(F32)).astype(BF16)):
+            expanded = jnp.where(picked, dot(piece, tile), 0.0).astype(BF16)
+            shift = shift + dot(expanded, value_up)
+        out_ref[:, h * 128 : (h + 1) * 128] = ((numerator + shift) / total).astype(BF16)
+
+    for copy in started:
+        copy.wait_send()
+    for j in range(4):
+        target = head * 4 + j
+
+        @pl.when(target != tp)
+        def _():
+            pltpu.make_async_remote_copy(
+                src_ref=fresh, dst_ref=fresh_in.at[slot], send_sem=f_send.at[j],
+                recv_sem=f_recv.at[slot], device_id=at(grp, target), device_id_type=MESH,
+            ).wait_send()
+
+    for j in range(4):
+        for g in range(2):
+
+            @pl.when(jnp.logical_not(jnp.logical_and(j == s, grp == g)))
+            def _():
+                pltpu.make_async_remote_copy(
+                    src_ref=psend.at[j, g], dst_ref=pbuf.at[mine], send_sem=p_send.at[j * 2 + g],
+                    recv_sem=p_recv.at[mine], device_id=at(g, z * 4 + j), device_id_type=MESH,
+                ).wait_send()
+
+
+def fused_device(
+    residual_input, input_norm_gain, query_weight, key_value_weight, shared_down_factors,
+    query_up_factors, key_value_up_factors, paged_base_keys, paged_base_values,
+    paged_down_factors, adapter_of_row, document_of_row, document_page_slots,
+):
+    rows, chunk = residual_input.shape
+    vmem = pl.BlockSpec(memory_space=pltpu.VMEM)
+    hbm = pl.BlockSpec(memory_space=pl.ANY)
+    smem = pl.BlockSpec(memory_space=pltpu.SMEM)
+    dma = pltpu.SemaphoreType.DMA
+    width = 16 * chunk
+    return pl.pallas_call(
+        fused_kernel,
+        out_shape=jax.ShapeDtypeStruct((rows, 256), BF16),
+        in_specs=[vmem, vmem, hbm, hbm, hbm, vmem, vmem, hbm, hbm, vmem, vmem, vmem, smem],
+        out_specs=vmem,
+        scratch_shapes=[
+            pltpu.VMEM((16, rows, chunk), BF16),
+            pltpu.VMEM((width, 256), BF16),
+            pltpu.VMEM((width, 64), BF16),
+            pltpu.VMEM((width, 48), BF16),
+            pltpu.VMEM((width, 128), BF16),
+            pltpu.VMEM((rows, 256), F32),
+            pltpu.VMEM((rows, 128), F32),
+            pltpu.VMEM((rows, 1), F32),
+            pltpu.VMEM((4, 4, 128, 128), BF16),
+            pltpu.VMEM((4, 4, 128, 128), BF16),
+            pltpu.VMEM((4, 128, 128), BF16),
+            pltpu.VMEM((8, rows, 384), BF16),
+            pltpu.VMEM((4, 4 * rows, 256), BF16),
+            pltpu.VMEM((512, 256), BF16),
+            pltpu.VMEM((512, 256), BF16),
+            pltpu.VMEM((4, 4 * rows, 256), F32),
+            pltpu.VMEM((4, 4 * rows, 1), F32),
+            pltpu.VMEM((4, 2, rows, 384), BF16),
+            pltpu.VMEM((8, rows, 384), BF16),
+            pltpu.VMEM((rows, 128), BF16),
+            pltpu.VMEM((4, rows, 128), BF16),
+            dma((5,)), dma((16,)), dma((16,)), dma((9,)), dma((12,)),
+            dma((7,)), dma((8,)), dma((4,)), dma((4,)), dma((8,)), dma((8,)),
+        ],
+        compiler_params=pltpu.CompilerParams(
+            collective_id=0, has_side_effects=True, vmem_limit_bytes=48 * 1024 * 1024
+        ),
+        cost_estimate=pl.CostEstimate(
+            flops=5_000_000_000, bytes_accessed=8_000_000, transcendentals=4_500_000
+        ),
+    )(
+        residual_input, input_norm_gain.reshape(16, chunk), query_weight, key_value_weight,
+        shared_down_factors, query_up_factors, key_value_up_factors, paged_base_keys,
+        paged_base_values, paged_down_factors, adapter_of_row.reshape(rows, 1),
+        document_of_row, document_page_slots,
+    )
 
 
 def merge_slices(numerator, factor_sum, maxima, totals):
@@ -264,6 +695,7 @@
         P(),
     )
     out_specs = P("grp", "tp")
+    fits = mesh.shape["grp"] == 2 and mesh.shape["tp"] == 16
     return jax.shard_map(
-        per_device, mesh=mesh, in_specs=in_specs, out_specs=out_specs, check_vma=False
-    )
+        fused_device if fits else per_device, mesh=mesh, in_specs=in_specs, out_specs=out_specs, check_vma=False
+    )

time: 368 us -> 85.8 us (0.23)
  waiting for transfers between devices: 116 us -> 0 us
  Pallas kernels: 0 us -> 74.1 us
  blocking collectives: 68 us -> 0 us
  local copies, waits for them, and re-layouts: 64.4 us -> 11.2 us
  starting transfers between devices: 48.3 us -> 0 us
  matrix products: 40 us -> 0 us
  other arithmetic: 14.9 us -> 0 us
  between operations: 13.8 us -> 0.08 us
    pallas_call x0 -> x1, Pallas kernels: none -> 74.1 us  [fused_device(): pl.pallas_call(fused_kernel, out_shape=jax.ShapeDtypeStruct((rows, 256),...]
    all_gather x2 -> x0, blocking collectives: 68 us -> none  [the longest x1 49.9 us: per_device(): lax.all_gather(kv_part, 'tp', axis=1, tiled=True)]
    all_to_all x10 -> x0, waiting for transfers between devices: 66.5 us -> none  [the longest x1 38.4 us: per_device(): lax.all_to_all(numerator.reshape(grp_count, per_source, all_heads, head_s...]
    all_gather x2 -> x0, waiting for transfers between devices: 49.2 us -> none  [the longest x1 38.6 us: per_device(): lax.all_gather(residual_input, 'tp', axis=1, tiled=True).astype(jnp.float32)]
    all_to_all x10 -> x0, starting transfers between devices: 48.3 us -> none  [the longest x1 7.63 us: per_device(): lax.all_to_all(maxima[:, :, None], 'tp', split_axis=1, concat_axis=2, til...]
    dot_general x24 -> x0, matrix products: 40 us -> none  [the longest x4 10.8 us: one_head(): jnp.einsum('ngl,ld->ngd', rounded, value_one, preferred_element_type=jnp....]
    gather x8 -> x0, local copies, waits for them, and re-layouts: 14.5 us -> none  [the longest x4 8.72 us: per_device(): piece.reshape((grp_count * capacity,) + piece.shape[2:])[slot_of]]
    another operation x8 -> x0, local copies, waits for them, and re-layouts: 11.9 us -> none  [the longest x1 6.59 us: per_device(): numerator.reshape(grp_count, per_source, all_heads, head_size)]
  transfers between devices with their start and end apart: 12 -> 0, of which waited for: 10 -> 0; matrix products, arithmetic and copies ran while one was open for 18% -> 0% of each run, Pallas kernels for 0% -> 0%
where the time goes in v1:
time: 85.8 us; the launch traced here: 85.3 us
  Pallas kernels  74.1 us (86%)
  local copies, waits for them, and re-layouts  11.2 us (13%)
    pallas_call x1, Pallas kernels, fused_device(): pl.pallas_call(fused_kernel, out_shape=jax.ShapeDtypeStruct((rows, 256),...  74.1 us
    unnamed x16, local copies, waits for them, and re-layouts  9.61 us

profile of v1, /device:TPU:9, one launch (start us, length us, event | category | flops | bytes accessed | tf_op | source)
XLA Modules:
  0.0 85.3 jit_solution(4851477003417658089)
XLA Ops:
  0.0 0.8 reshape.6.gain_ref
  0.8 0.8 copy.18.adapter_ref
  1.6 0.8 copy.19.doc_ref
  2.3 1.0 %copy.14.x_ref = bf16[128,320]{1,0:T(8,128)(2,1)S(1)} copy(bf16[128,320]{0,1:T(8,128)(2,1)} %param.13) | data formatting | bytes 163840 | tf_op args[0]
  3.3 0.9 %copy.17.d_ref = bf16[4,128,32]{2,1,0:T(8,128)(2,1)S(1)} copy(bf16[4,128,32]{1,2,0:T(8,128)(2,1)} %param.22) | data formatting | bytes 65536 | tf_op args[9]
  4.2 1.7 %copy.15.kvw_hbm = bf16[5120,64]{1,0:T(8,128)(2,1)S(1)} copy(bf16[5120,64]{0,1:T(8,128)(2,1)} %param.16) | data formatting | bytes 1310720 | tf_op args[3]
  5.9 0.0 copy-start
  5.9 0.0 copy-start.4
  5.9 1.7 %copy.16.dn_hbm = bf16[5120,48]{1,0:T(8,128)(2,1)S(1)} copy(bf16[5120,48]{0,1:T(8,128)(2,1)} %param.17) | data formatting | bytes 983040 | tf_op args[4]
  7.6 0.0 copy-done
  7.6 0.0 copy-done.4
  7.6 0.0 copy-start.1
  7.6 1.0 %copy-done.1 = bf16[4,128,512]{2,1,0:T(8,128)(2,1)S(1)} copy-done((bf16[4,128,512]{2,1,0:T(8,128)(2,1)S(1)}, bf16[4,128,512]{2,1,0:T(8,128)(2,1)}, u32[]{:S(2)}) %copy-start.1) | copy-done | bytes 524312
  8.7 0.0 copy-start.2
  8.7 1.0 %copy-done.2 = bf16[4,128,512]{2,1,0:T(8,128)(2,1)S(1)} copy-done((bf16[4,128,512]{2,1,0:T(8,128)(2,1)S(1)}, bf16[4,128,512]{2,1,0:T(8,128)(2,1)}, u32[]{:S(2)}) %copy-start.2) | copy-done | bytes 524312
  9.7 0.0 copy-start.3
  9.7 0.9 %copy-done.3 = bf16[16,16,256]{2,1,0:T(8,128)(2,1)S(1)} copy-done((bf16[16,16,256]{2,1,0:T(8,128)(2,1)S(1)}, bf16[16,16,256]{2,1,0:T(8,128)(2,1)}, u32[]{:S(2)}) %copy-start.3) | copy-done | bytes 131096
  10.6 74.1 %shard_map.127 = bf16[128,256]{1,0:T(8,128)(2,1)S(1)} custom-call(bf16[128,320]{1,0:T(8,128)(2,1)S(1)} %copy.14.x_ref, f32[16,320]{1,0:T(8,128)S(1)} %reshape.6.gain_ref, bf16[5120,256]{1,0:T(8,128)(2,1)} %qw_hbm.1, bf16[5120,64]{1,0:T(8,128)(2,1)S(1)} %copy.15.kvw_hbm, bf16[5120,48]{1,0:T(8,128)(2,1)S(1)} %copy.16.dn_hbm, ...), custom_call_target="tpu_custom_call" | custom-call | flops 5000000000 | bytes 8000000 | tf_op jit(solution)/shard_map/pallas_call | solution.py:396
  84.7 0.6 copy.21
Async XLA Ops:
  5.9 1.7 %copy-start = (bf16[16,16,1024]{2,1,0:T(8,128)(2,1)S(1)}, bf16[16,16,1024]{2,1,0:T(8,128)(2,1)}, u32[]{:S(2)}) copy-start(bf16[16,16,1024]{2,1,0:T(8,128)(2,1)} %ku_ref.1) | copy-start | bytes 1572868
  5.9 1.7 %copy-start.4 = (s32[2,64]{1,0:T(2,128)S(1)}, s32[2,64]{1,0:T(2,128)}, u32[]{:S(2)}) copy-start(s32[2,64]{1,0:T(2,128)} %slots_ref.1) | copy-start | bytes 1540
  7.6 1.0 %copy-start.1 = (bf16[4,128,512]{2,1,0:T(8,128)(2,1)S(1)}, bf16[4,128,512]{2,1,0:T(8,128)(2,1)}, u32[]{:S(2)}) copy-start(bf16[4,128,512]{2,1,0:T(8,128)(2,1)} %k_hbm.1) | copy-start | bytes 1572868
  8.7 1.0 %copy-start.2 = (bf16[4,128,512]{2,1,0:T(8,128)(2,1)S(1)}, bf16[4,128,512]{2,1,0:T(8,128)(2,1)}, u32[]{:S(2)}) copy-start(bf16[4,128,512]{2,1,0:T(8,128)(2,1)} %v_hbm.1) | copy-start | bytes 1572868
  9.7 0.9 %copy-start.3 = (bf16[16,16,256]{2,1,0:T(8,128)(2,1)S(1)}, bf16[16,16,256]{2,1,0:T(8,128)(2,1)}, u32[]{:S(2)}) copy-start(bf16[16,16,256]{2,1,0:T(8,128)(2,1)} %qu_ref.1) | copy-start | bytes 393220

commit v2 on v1

--- a/solution.py
+++ b/solution.py
@@ -34,14 +34,13 @@
 
 
 def fused_kernel(
-    x_ref, gain_ref, qw_hbm, kvw_hbm, dn_hbm, qu_ref, ku_ref, k_hbm, v_hbm, d_ref,
+    x_ref, gain_ref, qw_hbm, kvw_hbm, dn_hbm, qu_hbm, ku_hbm, k_hbm, v_hbm, d_ref,
     adapter_ref, doc_ref, slots_ref, out_ref,
-    xbuf, qw, kvw, dn, wo, yq, yo, ssq, kbuf, vbuf, dbuf, qbuf, lhs, kaug, vaug,
+    xbuf, qw, kvw, dn, qu_ref, ku_ref, wo, yq, yo, ssq, kbuf, vbuf, dbuf, qbuf, lhs, kaug, vaug,
     acc, peak, psend, pbuf, fresh, fresh_in,
     load_sem, x_send, x_recv, kv_send, kv_recv, q_send, q_recv, f_send, f_recv, p_send, p_recv,
 ):
-    rows = x_ref.shape[0]
-    chunk = x_ref.shape[1]
+    chunk, rows = x_ref.shape
     width = 16 * chunk
     grp = lax.axis_index("grp")
     tp = lax.axis_index("tp")
@@ -63,7 +62,8 @@
         for i, (src, dst) in enumerate(
             ((kvw_hbm, kvw), (dn_hbm, dn), (qw_hbm, qw),
              (k_hbm.at[:, :, pl.ds(pl.multiple_of(z * 128, 128), 128)], kbuf.at[z]),
-             (v_hbm.at[:, :, pl.ds(pl.multiple_of(z * 128, 128), 128)], vbuf.at[z]))
+             (v_hbm.at[:, :, pl.ds(pl.multiple_of(z * 128, 128), 128)], vbuf.at[z]),
+             (qu_hbm, qu_ref), (ku_hbm, ku_ref))
         )
     ]
     for load in loads:
@@ -74,8 +74,18 @@
         pl.semaphore_signal(barrier, inc=1, device_id=at(grp, (tp + i) % 16), device_id_type=MESH)
     for j in range(4):
         pl.semaphore_signal(barrier, inc=1, device_id=at(1 - grp, z * 4 + j), device_id_type=MESH)
-    xbuf[tp] = x_ref[...]
-    dbuf[z] = jnp.concatenate([d_ref[p] for p in range(4)], axis=1)
+    dbuf[z] = d_ref[...].reshape(128, 128).T
+    gain = jnp.zeros((1, chunk), F32)
+    for t in range(16):
+        gain = gain + jnp.where(tp == t, gain_ref[:, t * chunk : (t + 1) * chunk], 0.0)
+    x_rows = x_ref[...].T.astype(F32)
+    pieces = split_three(jnp.sum(x_rows * x_rows, axis=-1, keepdims=True))
+    xbuf[tp, :, :chunk] = (x_rows * gain).astype(BF16)
+    spare = lanes((rows, 384 - chunk))
+    sums = jnp.zeros(spare.shape, F32)
+    for i, piece in enumerate(pieces):
+        sums = jnp.where(spare == i, piece, sums)
+    xbuf[tp, :, chunk:] = sums.astype(BF16)
     pl.semaphore_wait(barrier, 19)
 
     started = []
@@ -99,39 +109,11 @@
         started.append(copy)
         return copy
 
-    first = [send_x(tp, i, at(grp, zo * 4 + s)) for i, zo in enumerate(z_others)]
+    send_x(tp, 0, at(grp, z_others[1] * 4 + s))
+    send_x(tp, 1, at(grp, z_others[0] * 4 + s))
     send_x(tp, 3, across)
     send_x(tp, 7, sibling)
-
-    loads[0].wait()
-    loads[1].wait()
-
-    def join(i, carry):
-        part = pl.ds(pl.multiple_of(i * chunk, 64), chunk)
-        wo[part, :] = jnp.concatenate(
-            [kvw[part, :], dn[part, :], jnp.zeros((chunk, 16), BF16)], axis=1
-        )
-        return carry
-
-    lax.fori_loop(0, 16, join, 0)
-    yq[...] = jnp.zeros_like(yq)
-    yo[...] = jnp.zeros_like(yo)
-    ssq[...] = jnp.zeros_like(ssq)
-    loads[2].wait()
-
-    def project(t):
-        block = xbuf[t].astype(F32)
-        ssq[...] += jnp.sum(block * block, axis=-1, keepdims=True)
-        scaled = (block * gain_ref[pl.ds(t, 1), :]).astype(BF16)
-        part = pl.ds(pl.multiple_of(t * chunk, 64), chunk)
-        yq[...] += dot(scaled, qw[part, :])
-        yo[...] += dot(scaled, wo[part, :])
-
-    project(tp)
-    for copy in first:
-        copy.wait_send()
-        started.remove(copy)
-    for n, i in enumerate((1, 2, 0)):
+    for i in (1, 2, 0):
         zo = z_others[i]
         cols = pl.ds(pl.multiple_of(zo * 128, 128), 128)
         device = at(grp, zo * 4 + s)
@@ -141,9 +123,35 @@
             started.append(
                 send(src, dst.at[z], kv_send.at[i * 3 + n2], kv_recv.at[z * 3 + n2], device)
             )
-    for i, zo in enumerate(z_others):
-        t = zo * 4 + s
+
+    loads[0].wait()
+    loads[1].wait()
+
+    def join(i, carry):
+        part = pl.ds(pl.multiple_of(i * 128, 128), 128)
+        both = jnp.concatenate([kvw[:, part], dn[:, part], jnp.zeros((16, 128), BF16)], axis=0)
+        wo[part, :] = both.T
+        return carry
+
+    lax.fori_loop(0, width // 128, join, 0)
+    yq[...] = jnp.zeros_like(yq)
+    yo[...] = jnp.zeros_like(yo)
+    ssq[...] = jnp.zeros_like(ssq)
+    loads[2].wait()
+
+    def project(t):
+        scaled = xbuf[t, :, :chunk]
+        ssq[...] += jnp.sum(xbuf[t, :, chunk:].astype(F32), axis=-1, keepdims=True)
+        part = pl.ds(pl.multiple_of(t * chunk, 64), chunk)
+        yq[...] += dot(scaled, qw[part, :])
+        yo[...] += dot(scaled, wo[part, :])
+
+    project(tp)
+    for i in (1, 0, 2):
+        t = z_others[i] * 4 + s
         arrive(xbuf.at[t], x_send.at[0], x_recv.at[t])
+        if i == 1:
+            send_x(t, 2, at(grp, z_others[0] * 4 + s))
         send_x(t, 4 + i, across)
         send_x(t, 8 + i, sibling)
         project(t)
@@ -161,7 +169,13 @@
     rinv = lax.rsqrt(ssq[...] * (1.0 / width) + 1e-06)
     other = yo[...] * rinv
     low = other[:, 64:128].astype(BF16)
-    adapter = adapter_ref[...]
+    def column(row_ref):
+        return jnp.broadcast_to(row_ref[...].astype(F32), (rows, rows)).T.astype(jnp.int32)
+
+    adapter = column(adapter_ref)
+    adapter = jnp.concatenate([adapter, adapter], axis=1)
+    loads[5].wait()
+    loads[6].wait()
     wide = lanes((rows, 256))
     picked = (wide // 16) == adapter
     row_of = lax.broadcasted_iota(jnp.int32, (64, 256), 0)
@@ -319,10 +333,10 @@
         index = (mine + n) % 8
         arrive(pbuf.at[index], x_send.at[0], p_recv.at[index])
     half = slots_ref.shape[1]
-    document = doc_ref[...]
+    document = column(doc_ref)
     holder = jnp.where(document == 0, slots_ref[0, 0] // half, slots_ref[1, 0] // half)
+    holder = jnp.concatenate([holder] * 3, axis=1)
     narrow = lanes((rows, 128))
-    picked = (lanes((rows, 256)) // 16) == adapter_ref[...]
     value_up = ku_ref[:, :, pl.ds(pl.multiple_of(512 + z * 128, 128), 128)].reshape(256, 128)
     row_of = lax.broadcasted_iota(jnp.int32, (128, 256), 0)
     tile = (row_of == lanes((128, 256)) % 16).astype(F32).astype(BF16)
@@ -389,20 +403,22 @@
 ):
     rows, chunk = residual_input.shape
     vmem = pl.BlockSpec(memory_space=pltpu.VMEM)
-    hbm = pl.BlockSpec(memory_space=pl.ANY)
+    hbm = pl.BlockSpec(memory_space=pltpu.HBM)
     smem = pl.BlockSpec(memory_space=pltpu.SMEM)
     dma = pltpu.SemaphoreType.DMA
     width = 16 * chunk
     return pl.pallas_call(
         fused_kernel,
         out_shape=jax.ShapeDtypeStruct((rows, 256), BF16),
-        in_specs=[vmem, vmem, hbm, hbm, hbm, vmem, vmem, hbm, hbm, vmem, vmem, vmem, smem],
+        in_specs=[vmem, vmem, hbm, hbm, hbm, hbm, hbm, hbm, hbm, vmem, vmem, vmem, smem],
         out_specs=vmem,
         scratch_shapes=[
-            pltpu.VMEM((16, rows, chunk), BF16),
+            pltpu.VMEM((16, rows, 384), BF16),
             pltpu.VMEM((width, 256), BF16),
-            pltpu.VMEM((width, 64), BF16),
-            pltpu.VMEM((width, 48), BF16),
+            pltpu.VMEM((64, width), BF16),
+            pltpu.VMEM((48, width), BF16),
+            pltpu.VMEM((16, 16, 256), BF16),
+            pltpu.VMEM((16, 16, 1024), BF16),
             pltpu.VMEM((width, 128), BF16),
             pltpu.VMEM((rows, 256), F32),
             pltpu.VMEM((rows, 128), F32),
@@ -420,20 +436,20 @@
             pltpu.VMEM((8, rows, 384), BF16),
             pltpu.VMEM((rows, 128), BF16),
             pltpu.VMEM((4, rows, 128), BF16),
-            dma((5,)), dma((16,)), dma((16,)), dma((9,)), dma((12,)),
+            dma((7,)), dma((16,)), dma((16,)), dma((9,)), dma((12,)),
             dma((7,)), dma((8,)), dma((4,)), dma((4,)), dma((8,)), dma((8,)),
         ],
         compiler_params=pltpu.CompilerParams(
-            collective_id=0, has_side_effects=True, vmem_limit_bytes=48 * 1024 * 1024
+            collective_id=0, has_side_effects=True, vmem_limit_bytes=63 * 1024 * 1024
         ),
         cost_estimate=pl.CostEstimate(
             flops=5_000_000_000, bytes_accessed=8_000_000, transcendentals=4_500_000
         ),
     )(
-        residual_input, input_norm_gain.reshape(16, chunk), query_weight, key_value_weight,
-        shared_down_factors, query_up_factors, key_value_up_factors, paged_base_keys,
-        paged_base_values, paged_down_factors, adapter_of_row.reshape(rows, 1),
-        document_of_row, document_page_slots,
+        residual_input.T, input_norm_gain.reshape(1, width), query_weight, key_value_weight.T,
+        shared_down_factors.T, query_up_factors, key_value_up_factors, paged_base_keys,
+        paged_base_values, paged_down_factors.transpose(0, 2, 1), adapter_of_row.reshape(1, rows),
+        document_of_row.reshape(1, rows), document_page_slots,
     )
 
 

time: 85.8 us -> 80.5 us (0.938)
  the two profiles are of different devices: /device:TPU:9 before, /device:TPU:1 now
where the time goes in v2:
time: 80.5 us; the launch traced here: 80.3 us
  Pallas kernels  78.8 us (98%)
  local copies, waits for them, and re-layouts  1.47 us (2%)
    pallas_call x1, Pallas kernels, fused_device(): pl.pallas_call(fused_kernel, out_shape=jax.ShapeDtypeStruct((rows, 256),...  78.8 us

profile of v2, /device:TPU:1, one launch (start us, length us, event | category | flops | bytes accessed | tf_op | source)
XLA Modules:
  0.0 80.3 jit_solution(12465577788272438651)
XLA Ops:
  0.0 78.8 %shard_map.127 = bf16[128,256]{1,0:T(8,128)(2,1)} custom-call(bf16[320,128]{1,0:T(8,128)(2,1)} %bitcast.9, f32[1,5120]{1,0:T(1,128)} %bitcast.11, bf16[5120,256]{1,0:T(8,128)(2,1)} %qw_hbm.1, bf16[64,5120]{1,0:T(8,128)(2,1)} %bitcast.7, bf16[48,5120]{1,0:T(8,128)(2,1)} %bitcast.8, bf16[16,16,256]{2,1,0:T(8,128)(2,1)} %qu_hbm.1, ...), custom_call_target="tpu_custom_call" | custom-call | flops 5000000000 | bytes 8000000 | tf_op jit(solution)/shard_map/pallas_call | solution.py:410
  78.8 1.5 %copy.15 = bf16[128,256]{1,0:T(8,128)(2,1)} copy(bf16[128,256]{1,0:T(8,128)(2,1)} %shard_map.127) | data formatting | bytes 131072

commit v3 on v2

--- a/solution.py
+++ b/solution.py
@@ -36,7 +36,7 @@
 def fused_kernel(
     x_ref, gain_ref, qw_hbm, kvw_hbm, dn_hbm, qu_hbm, ku_hbm, k_hbm, v_hbm, d_ref,
     adapter_ref, doc_ref, slots_ref, out_ref,
-    xbuf, qw, kvw, dn, qu_ref, ku_ref, wo, yq, yo, ssq, kbuf, vbuf, dbuf, qbuf, lhs, kaug, vaug,
+    xbuf, qw, kvw, dn, qu_ref, ku_ref, wo, yq, yo, ssq, kbuf, vbuf, dbuf, qbuf, qcol, kaug, vaug, vup,
     acc, peak, psend, pbuf, fresh, fresh_in,
     load_sem, x_send, x_recv, kv_send, kv_recv, q_send, q_recv, f_send, f_recv, p_send, p_recv,
 ):
@@ -74,7 +74,7 @@
         pl.semaphore_signal(barrier, inc=1, device_id=at(grp, (tp + i) % 16), device_id_type=MESH)
     for j in range(4):
         pl.semaphore_signal(barrier, inc=1, device_id=at(1 - grp, z * 4 + j), device_id_type=MESH)
-    dbuf[z] = d_ref[...].reshape(128, 128).T
+    dbuf[z] = d_ref[...].reshape(128, 128)
     gain = jnp.zeros((1, chunk), F32)
     for t in range(16):
         gain = gain + jnp.where(tp == t, gain_ref[:, t * chunk : (t + 1) * chunk], 0.0)
@@ -108,6 +108,9 @@
         copy = send(xbuf.at[t], xbuf.at[t], x_send.at[sem], x_recv.at[t], device)
         started.append(copy)
         return copy
+
+    def send_q(index, sem, device):
+        started.append(send(qbuf.at[index], qbuf.at[index], q_send.at[sem], q_recv.at[index], device))
 
     send_x(tp, 0, at(grp, z_others[1] * 4 + s))
     send_x(tp, 1, at(grp, z_others[0] * 4 + s))
@@ -146,7 +149,43 @@
         yq[...] += dot(scaled, qw[part, :])
         yo[...] += dot(scaled, wo[part, :])
 
+    def augment(zo):
+        down = dbuf[zo].astype(F32).T.astype(BF16)
+        for p in range(4):
+            part = pl.ds(p * 128, 128)
+            kaug[zo, part, :128] = kbuf[zo, p]
+            kaug[zo, part, 128:] = jnp.concatenate(
+                [down[:, p * 32 : p * 32 + 16], jnp.zeros((128, 112), BF16)], axis=1
+            )
+            vaug[zo, :128, part] = vbuf[zo, p].T
+            vaug[zo, 128:144, part] = dbuf[zo, p * 32 + 16 : p * 32 + 32, :]
+        first_row = lax.broadcasted_iota(jnp.int32, (16, 512), 0) == 0
+        vaug[zo, 144:, :] = first_row.astype(F32).astype(BF16)
+
+    def attend(zo, j, start):
+        scores = dot(kaug[zo], qcol[j])
+        top = jnp.max(scores, axis=0, keepdims=True) * scale
+        if not start:
+            old = peak[j]
+            top = jnp.maximum(old, top)
+        weights = jnp.exp2(scores * scale - top).astype(BF16)
+        product = dot(vaug[zo], weights)
+        if start:
+            acc[j] = product
+        else:
+            acc[j] = acc[j] * jnp.exp2(old - top) + product
+        peak[j] = top
+
     project(tp)
+    loads[3].wait()
+    loads[4].wait()
+    loads[5].wait()
+    loads[6].wait()
+    augment(z)
+    qcol[:, 144:, :] = jnp.zeros((4, 112, 512), BF16)
+    vup[...] = (
+        ku_ref[:, :, pl.ds(pl.multiple_of(512 + z * 128, 128), 128)].reshape(256, 128).T
+    )
     for i in (1, 0, 2):
         t = z_others[i] * 4 + s
         arrive(xbuf.at[t], x_send.at[0], x_recv.at[t])
@@ -174,8 +213,6 @@
 
     adapter = column(adapter_ref)
     adapter = jnp.concatenate([adapter, adapter], axis=1)
-    loads[5].wait()
-    loads[6].wait()
     wide = lanes((rows, 256))
     picked = (wide // 16) == adapter
     row_of = lax.broadcasted_iota(jnp.int32, (64, 256), 0)
@@ -192,9 +229,8 @@
     pair_cols = pl.ds(pl.multiple_of((tp // 2) * 128, 128), 128)
     kv_update = dot(kv_low, ku_ref[:, :, pair_cols].reshape(256, 128))
     kv_base = other[:, :64]
-    kv_full = jnp.concatenate([kv_base, kv_base], axis=1) + kv_update
-    narrow = lanes((rows, 128))
-    fresh[...] = jnp.where((narrow // 64) == odd, kv_full, 0.0).astype(BF16)
+    kv_full = (jnp.concatenate([kv_base, kv_base], axis=1) + kv_update).T
+    fresh[...] = jnp.where(odd == 1, kv_full[64:], kv_full[:64]).astype(BF16)
     fold_row = lax.broadcasted_iota(jnp.int32, (256, 128), 0) % 16
     fold_col = lanes((256, 128))
     key_up = ku_ref[:, :, pl.ds(pl.multiple_of(z * 128, 128), 128)].reshape(256, 128)
@@ -205,14 +241,14 @@
         fold = (fold_col == fold_row + 16 * h).astype(F32).astype(BF16)
         factors = factors + dot(full, fold)
     mine = 4 * grp + s
-    qbuf[mine, :, :256] = queries
-    qbuf[mine, :, 256:] = factors.astype(BF16)
-
-    n = 0
-    for g, shift in ((1 - grp, 0), (1 - grp, 1), (1 - grp, 2), (1 - grp, 3), (grp, 1), (grp, 2), (grp, 3)):
-        device = at(g, z * 4 + (s + shift) % 4)
-        started.append(send(qbuf.at[mine], qbuf.at[mine], q_send.at[n], q_recv.at[mine], device))
-        n += 1
+    qbuf[mine, :256, :] = queries.astype(F32).T.astype(BF16)
+    qbuf[mine, 256:, :] = factors.T[:32].astype(BF16)
+
+    far = (1 - y) * 2 + c
+    direct = [(grp, far), (1 - grp, s), (1 - grp, far)]
+    for n, (g, j) in enumerate(direct):
+        send_q(mine, n, at(g, z * 4 + j))
+    send_q(mine, 3, sibling)
     head = (tp % 8) // 2
     slot = (tp // 8) * 2 + odd
     for j in range(4):
@@ -226,50 +262,20 @@
         def _():
             fresh_in[slot] = fresh[...]
 
-    def augment(zo):
-        for p in range(4):
-            part = pl.ds(p * 128, 128)
-            down = dbuf[zo, :, p * 32 : (p + 1) * 32]
-            kaug[part, :128] = kbuf[zo, p]
-            kaug[part, 128:] = jnp.concatenate(
-                [down[:, :16], down[:, :16], jnp.zeros((128, 96), BF16)], axis=1
-            )
-            right = jnp.concatenate([down[:, 16:], jnp.zeros((128, 112), BF16)], axis=1)
-            vaug[part, :128] = vbuf[zo, p]
-            vaug[part, 128:] = jnp.where(
-                lanes((128, 128)) == 16, 1.0, right.astype(F32)
-            ).astype(BF16)
-
-    def attend(j, start):
-        scores = dot_nt(lhs[j], kaug[...]) * scale
-        top = jnp.max(scores, axis=-1, keepdims=True)
-        if not start:
-            old = peak[j]
-            top = jnp.maximum(old, top)
-        weights = jnp.exp2(scores - top).astype(BF16)
-        product = dot(weights, vaug[...])
-        if start:
-            acc[j] = product
-        else:
-            acc[j] = acc[j] * jnp.exp2(old - top) + product
-        peak[j] = top
-
-    loads[3].wait()
-    loads[4].wait()
-    augment(z)
-    f_lane = lanes((rows, 128)) // 16
-    for shift in range(4):
-        j = (s + shift) % 4
-        for g, local in ((grp, True), (1 - grp, False)):
+    for n, (g, j) in enumerate(direct):
+        index = 4 * g + j
+        arrive(qbuf.at[index], x_send.at[0], q_recv.at[index])
+        send_q(index, 4 + n, sibling)
+    for j, waited in ((s, True), (far, True), (y * 2 + 1 - c, False), (3 - s, False)):
+        for g in (grp, 1 - grp):
             index = 4 * g + j
-            if not (local and shift == 0):
+            if not waited:
                 arrive(qbuf.at[index], x_send.at[0], q_recv.at[index])
-            extra = qbuf[index, :, 256:].astype(F32)
             for h in range(2):
                 part = pl.ds(pl.multiple_of(h * 256 + g * 128, 128), 128)
-                lhs[j, part, :128] = qbuf[index, :, h * 128 : (h + 1) * 128]
-                lhs[j, part, 128:] = jnp.where(f_lane == h, extra, 0.0).astype(BF16)
-        attend(j, True)
+                qcol[j, :128, part] = qbuf[index, h * 128 : (h + 1) * 128, :]
+                qcol[j, 128:144, part] = qbuf[index, 256 + h * 16 : 272 + h * 16, :]
+        attend(z, j, True)
 
     def arrived(zo):
         for n2, dst in enumerate((kbuf, vbuf, dbuf)):
@@ -280,7 +286,7 @@
         augment(zo)
 
         def body(j, carry):
-            attend(j, False)
+            attend(zo, j, False)
             return carry
 
         lax.fori_loop(0, 4, body, 0)
@@ -290,22 +296,18 @@
 
     def last(shift, carry):
         j = (s + shift) % 4
-        attend(j, False)
-        lane = lanes((128, 128))
+        attend(z_others[2], j, False)
+        line = lax.broadcasted_iota(jnp.int32, (16, 128), 0)
         for g in range(2):
-            stats = None
             for h in range(2):
                 part = pl.ds(h * 256 + g * 128, 128)
-                psend[j, g, :, h * 128 : (h + 1) * 128] = acc[j, part, :128].astype(BF16)
-                tail = acc[j, part, 128:]
-                high = tail.astype(BF16).astype(F32)
-                m0, m1, m2 = split_three(peak[j, part, :])
-                one = high + pltpu.roll(tail - high, 32, 1)
-                one = jnp.where(lane == 24, m0, one)
-                one = jnp.where(lane == 25, m1, one)
-                one = jnp.where(lane == 26, m2, one)
-                stats = one if h == 0 else stats + pltpu.roll(one, 64, 1)
-            psend[j, g, :, 256:] = stats.astype(BF16)
+                psend[j, g, h * 128 : (h + 1) * 128, :] = acc[j, :128, part].astype(BF16)
+                psend[j, g, 256 + h * 32 : 272 + h * 32, :] = acc[j, 128:144, part].astype(BF16)
+                stats = jnp.zeros((16, 128), F32)
+                pieces = split_three(acc[j, 144:145, part])[:2] + split_three(peak[j, :, part])
+                for i, piece in enumerate(pieces):
+                    stats = jnp.where(line == i, piece, stats)
+                psend[j, g, 272 + h * 32 : 288 + h * 32, :] = stats.astype(BF16)
             here = jnp.logical_and(j == s, grp == g)
 
             @pl.when(jnp.logical_not(here))
@@ -327,51 +329,37 @@
         def _():
             arrive(fresh_in.at[n], x_send.at[0], f_recv.at[n])
 
-    own_key = fresh_in[0].astype(F32) + fresh_in[1].astype(F32)
-    own_value = fresh_in[2].astype(F32) + fresh_in[3].astype(F32)
+    own_key = jnp.concatenate([fresh_in[0], fresh_in[1]], axis=0).astype(F32)
+    own_value = jnp.concatenate([fresh_in[2], fresh_in[3]], axis=0).astype(F32)
     for n in range(1, 8):
         index = (mine + n) % 8
         arrive(pbuf.at[index], x_send.at[0], p_recv.at[index])
     half = slots_ref.shape[1]
-    document = column(doc_ref)
-    holder = jnp.where(document == 0, slots_ref[0, 0] // half, slots_ref[1, 0] // half)
-    holder = jnp.concatenate([holder] * 3, axis=1)
-    narrow = lanes((rows, 128))
-    value_up = ku_ref[:, :, pl.ds(pl.multiple_of(512 + z * 128, 128), 128)].reshape(256, 128)
-    row_of = lax.broadcasted_iota(jnp.int32, (128, 256), 0)
-    tile = (row_of == lanes((128, 256)) % 16).astype(F32).astype(BF16)
+    holder = jnp.where(doc_ref[...] == 0, slots_ref[0, 0] // half, slots_ref[1, 0] // half)
+    picked = lax.broadcasted_iota(jnp.int32, (256, rows), 0) // 16 == adapter_ref[...]
     blocks = [
         jnp.where(holder == 0, pbuf[j].astype(F32), pbuf[4 + j].astype(F32)) for j in range(4)
     ]
     for h in range(2):
-        query = qbuf[mine, :, h * 128 : (h + 1) * 128].astype(F32)
-        own = jnp.sum(query * own_key, axis=-1, keepdims=True) * scale
+        query = qbuf[mine, h * 128 : (h + 1) * 128, :].astype(F32)
+        own = jnp.sum(query * own_key, axis=0, keepdims=True) * scale
+        base = 256 + h * 32
+        peaks = [b[base + 18 : base + 19] + b[base + 19 : base + 20] + b[base + 20 : base + 21] for b in blocks]
         top = own
-        parts = []
-        for block in blocks:
-            stats = block[:, 256:]
-            if h:
-                stats = pltpu.roll(stats, 64, 1)
-            at_peak = jnp.logical_and(narrow >= 24, narrow < 27)
-            m = jnp.sum(jnp.where(at_peak, stats, 0.0), axis=-1, keepdims=True)
-            tail = jnp.where(narrow < 17, stats + pltpu.roll(stats, 96, 1), 0.0)
+        for m in peaks:
             top = jnp.maximum(top, m)
-            parts.append((block[:, h * 128 : (h + 1) * 128], tail, m))
-        own_weight = jnp.exp2(own - top)
-        numerator = own_weight * own_value
-        tail_sum = jnp.zeros((rows, 128), F32)
-        for num, tail, m in parts:
+        total = jnp.exp2(own - top)
+        numerator = total * own_value
+        factor = jnp.zeros((16, rows), F32)
+        for block, m in zip(blocks, peaks):
             weight = jnp.exp2(m - top)
-            numerator = numerator + num * weight
-            tail_sum = tail_sum + tail * weight
-        total = jnp.sum(jnp.where(narrow == 16, tail_sum, 0.0), axis=-1, keepdims=True) + own_weight
-        factor = jnp.where(narrow < 16, tail_sum, 0.0)
-        high = factor.astype(BF16)
-        shift = jnp.zeros((rows, 128), F32)
-        for piece in (high, (factor - high.astype(F32)).astype(BF16)):
-            expanded = jnp.where(picked, dot(piece, tile), 0.0).astype(BF16)
-            shift = shift + dot(expanded, value_up)
-        out_ref[:, h * 128 : (h + 1) * 128] = ((numerator + shift) / total).astype(BF16)
+            numerator = numerator + block[h * 128 : (h + 1) * 128] * weight
+            factor = factor + block[base : base + 16] * weight
+            total = total + (block[base + 16 : base + 17] + block[base + 17 : base + 18]) * weight
+        expanded = jnp.where(picked, jnp.concatenate([factor] * 16, axis=0), 0.0)
+        high = expanded.astype(BF16)
+        shift = dot(vup[...], high) + dot(vup[...], (expanded - high.astype(F32)).astype(BF16))
+        out_ref[:, h * 128 : (h + 1) * 128] = ((numerator + shift) / total).T.astype(BF16)
 
     for copy in started:
         copy.wait_send()
@@ -426,16 +414,17 @@
             pltpu.VMEM((4, 4, 128, 128), BF16),
             pltpu.VMEM((4, 4, 128, 128), BF16),
             pltpu.VMEM((4, 128, 128), BF16),
-            pltpu.VMEM((8, rows, 384), BF16),
-            pltpu.VMEM((4, 4 * rows, 256), BF16),
-            pltpu.VMEM((512, 256), BF16),
-            pltpu.VMEM((512, 256), BF16),
-            pltpu.VMEM((4, 4 * rows, 256), F32),
-            pltpu.VMEM((4, 4 * rows, 1), F32),
-            pltpu.VMEM((4, 2, rows, 384), BF16),
-            pltpu.VMEM((8, rows, 384), BF16),
-            pltpu.VMEM((rows, 128), BF16),
-            pltpu.VMEM((4, rows, 128), BF16),
+            pltpu.VMEM((8, 288, rows), BF16),
+            pltpu.VMEM((4, 256, 4 * rows), BF16),
+            pltpu.VMEM((4, 512, 256), BF16),
+            pltpu.VMEM((4, 160, 512), BF16),
+            pltpu.VMEM((128, 256), BF16),
+            pltpu.VMEM((4, 160, 4 * rows), F32),
+            pltpu.VMEM((4, 1, 4 * rows), F32),
+            pltpu.VMEM((4, 2, 320, rows), BF16),
+            pltpu.VMEM((8, 320, rows), BF16),
+            pltpu.VMEM((64, rows), BF16),
+            pltpu.VMEM((4, 64, rows), BF16),
             dma((7,)), dma((16,)), dma((16,)), dma((9,)), dma((12,)),
             dma((7,)), dma((8,)), dma((4,)), dma((4,)), dma((8,)), dma((8,)),
         ],

time: 80.5 us -> 67.2 us (0.83)
  the two profiles are of different devices: /device:TPU:1 before, /device:TPU:9 now
where the time goes in v3:
time: 67.2 us; the launch traced here: 66.4 us
  Pallas kernels  64.9 us (97%)
  local copies, waits for them, and re-layouts  1.47 us (2%)
    pallas_call x1, Pallas kernels, fused_device(): pl.pallas_call(fused_kernel, out_shape=jax.ShapeDtypeStruct((rows, 256),...  64.9 us
    unnamed x1, local copies, waits for them, and re-layouts  1.47 us

profile of v3, /device:TPU:9, one launch (start us, length us, event | category | flops | bytes accessed | tf_op | source)
XLA Modules:
  0.0 66.4 jit_solution(12064909019048900422)
XLA Ops:
  0.0 64.9 %shard_map.127 = bf16[128,256]{1,0:T(8,128)(2,1)} custom-call(bf16[320,128]{1,0:T(8,128)(2,1)} %bitcast.9, f32[1,5120]{1,0:T(1,128)} %bitcast.11, bf16[5120,256]{1,0:T(8,128)(2,1)} %qw_hbm.1, bf16[64,5120]{1,0:T(8,128)(2,1)} %bitcast.7, bf16[48,5120]{1,0:T(8,128)(2,1)} %bitcast.8, bf16[16,16,256]{2,1,0:T(8,128)(2,1)} %qu_hbm.1, ...), custom_call_target="tpu_custom_call" | custom-call | flops 5000000000 | bytes 8000000 | tf_op jit(solution)/shard_map/pallas_call | solution.py:398
  64.9 1.5 %copy.15 = bf16[128,256]{1,0:T(8,128)(2,1)} copy(bf16[128,256]{1,0:T(8,128)(2,1)} %shard_map.127) | data formatting | bytes 131072

commit v4 on v3

--- a/solution.py
+++ b/solution.py
@@ -116,15 +116,14 @@
     send_x(tp, 1, at(grp, z_others[0] * 4 + s))
     send_x(tp, 3, across)
     send_x(tp, 7, sibling)
-    for i in (1, 2, 0):
+    def send_kv(i):
         zo = z_others[i]
         cols = pl.ds(pl.multiple_of(zo * 128, 128), 128)
-        device = at(grp, zo * 4 + s)
-        for n2, (src, dst) in enumerate(
+        for n, (src, dst) in enumerate(
             ((k_hbm.at[:, :, cols], kbuf), (v_hbm.at[:, :, cols], vbuf), (dbuf.at[z], dbuf))
         ):
             started.append(
-                send(src, dst.at[z], kv_send.at[i * 3 + n2], kv_recv.at[z * 3 + n2], device)
+                send(src, dst.at[z], kv_send.at[i * 3 + n], kv_recv.at[z * 3 + n], at(grp, zo * 4 + s))
             )
 
     loads[0].wait()
@@ -193,7 +192,10 @@
             send_x(t, 2, at(grp, z_others[0] * 4 + s))
         send_x(t, 4 + i, across)
         send_x(t, 8 + i, sibling)
-        project(t)
+    send_kv(1)
+    send_kv(2)
+    for i in (1, 0, 2):
+        project(z_others[i] * 4 + s)
     for i, zo in enumerate([z] + z_others):
         t = zo * 4 + (1 - y) * 2 + c
         arrive(xbuf.at[t], x_send.at[0], x_recv.at[t])
@@ -262,6 +264,7 @@
         def _():
             fresh_in[slot] = fresh[...]
 
+    send_kv(0)
     for n, (g, j) in enumerate(direct):
         index = 4 * g + j
         arrive(qbuf.at[index], x_send.at[0], q_recv.at[index])
@@ -281,7 +284,7 @@
         for n2, dst in enumerate((kbuf, vbuf, dbuf)):
             arrive(dst.at[zo], x_send.at[0], kv_recv.at[zo * 3 + n2])
 
-    for zo in z_others[:2]:
+    for zo in z_others[1:]:
         arrived(zo)
         augment(zo)
 
@@ -291,12 +294,12 @@
 
         lax.fori_loop(0, 4, body, 0)
 
-    arrived(z_others[2])
-    augment(z_others[2])
+    arrived(z_others[0])
+    augment(z_others[0])
 
     def last(shift, carry):
         j = (s + shift) % 4
-        attend(z_others[2], j, False)
+        attend(z_others[0], j, False)
         line = lax.broadcasted_iota(jnp.int32, (16, 128), 0)
         for g in range(2):
             for h in range(2):

time: 67.2 us -> 57.3 us (0.85)
  Pallas kernels: 64.9 us -> 55.1 us
    pallas_call x1, Pallas kernels: 64.9 us -> 55.1 us  [fused_device(): pl.pallas_call(fused_kernel, out_shape=jax.ShapeDtypeStruct((rows, 256),...]
where the time goes in v4:
time: 57.3 us; the launch traced here: 56.5 us
  Pallas kernels  55.1 us (96%)
  local copies, waits for them, and re-layouts  1.47 us (3%)
    pallas_call x1, Pallas kernels, fused_device(): pl.pallas_call(fused_kernel, out_shape=jax.ShapeDtypeStruct((rows, 256),...  55.1 us
    unnamed x1, local copies, waits for them, and re-layouts  1.47 us

profile of v4, /device:TPU:9, one launch (start us, length us, event | category | flops | bytes accessed | tf_op | source)
XLA Modules:
  0.0 56.5 jit_solution(14771939046081111878)
XLA Ops:
  0.0 55.1 %shard_map.127 = bf16[128,256]{1,0:T(8,128)(2,1)} custom-call(bf16[320,128]{1,0:T(8,128)(2,1)} %bitcast.9, f32[1,5120]{1,0:T(1,128)} %bitcast.11, bf16[5120,256]{1,0:T(8,128)(2,1)} %qw_hbm.1, bf16[64,5120]{1,0:T(8,128)(2,1)} %bitcast.7, bf16[48,5120]{1,0:T(8,128)(2,1)} %bitcast.8, bf16[16,16,256]{2,1,0:T(8,128)(2,1)} %qu_hbm.1, ...), custom_call_target="tpu_custom_call" | custom-call | flops 5000000000 | bytes 8000000 | tf_op jit(solution)/shard_map/pallas_call | solution.py:401
  55.1 1.5 %copy.15 = bf16[128,256]{1,0:T(8,128)(2,1)} copy(bf16[128,256]{1,0:T(8,128)(2,1)} %shard_map.127) | data formatting | bytes 131072

commit v5 on v4

--- a/solution.py
+++ b/solution.py
@@ -193,7 +193,7 @@
         send_x(t, 4 + i, across)
         send_x(t, 8 + i, sibling)
     send_kv(1)
-    send_kv(2)
+    send_kv(0)
     for i in (1, 0, 2):
         project(z_others[i] * 4 + s)
     for i, zo in enumerate([z] + z_others):
@@ -264,7 +264,7 @@
         def _():
             fresh_in[slot] = fresh[...]
 
-    send_kv(0)
+    send_kv(2)
     for n, (g, j) in enumerate(direct):
         index = 4 * g + j
         arrive(qbuf.at[index], x_send.at[0], q_recv.at[index])
@@ -284,7 +284,7 @@
         for n2, dst in enumerate((kbuf, vbuf, dbuf)):
             arrive(dst.at[zo], x_send.at[0], kv_recv.at[zo * 3 + n2])
 
-    for zo in z_others[1:]:
+    for zo in z_others[:2]:
         arrived(zo)
         augment(zo)
 
@@ -294,12 +294,12 @@
 
         lax.fori_loop(0, 4, body, 0)
 
-    arrived(z_others[0])
-    augment(z_others[0])
+    arrived(z_others[2])
+    augment(z_others[2])
 
     def last(shift, carry):
         j = (s + shift) % 4
-        attend(z_others[0], j, False)
+        attend(z_others[2], j, False)
         line = lax.broadcasted_iota(jnp.int32, (16, 128), 0)
         for g in range(2):
             for h in range(2):

time: 57.3 us -> 55.8 us (0.974)
  Pallas kernels: 55.1 us -> 53.7 us
    pallas_call x1, Pallas kernels: 55.1 us -> 53.7 us  [fused_device(): pl.pallas_call(fused_kernel, out_shape=jax.ShapeDtypeStruct((rows, 256),...]
where the time goes in v5:
time: 55.8 us; the launch traced here: 55.2 us
  Pallas kernels  53.7 us (96%)
  local copies, waits for them, and re-layouts  1.47 us (3%)
    pallas_call x1, Pallas kernels, fused_device(): pl.pallas_call(fused_kernel, out_shape=jax.ShapeDtypeStruct((rows, 256),...  53.7 us
    unnamed x1, local copies, waits for them, and re-layouts  1.47 us

profile of v5, /device:TPU:9, one launch (start us, length us, event | category | flops | bytes accessed | tf_op | source)
XLA Modules:
  0.0 55.2 jit_solution(2522109505931318927)
XLA Ops:
  0.0 53.7 %shard_map.127 = bf16[128,256]{1,0:T(8,128)(2,1)} custom-call(bf16[320,128]{1,0:T(8,128)(2,1)} %bitcast.9, f32[1,5120]{1,0:T(1,128)} %bitcast.11, bf16[5120,256]{1,0:T(8,128)(2,1)} %qw_hbm.1, bf16[64,5120]{1,0:T(8,128)(2,1)} %bitcast.7, bf16[48,5120]{1,0:T(8,128)(2,1)} %bitcast.8, bf16[16,16,256]{2,1,0:T(8,128)(2,1)} %qu_hbm.1, ...), custom_call_target="tpu_custom_call" | custom-call | flops 5000000000 | bytes 8000000 | tf_op jit(solution)/shard_map/pallas_call | solution.py:401
  53.7 1.5 %copy.15 = bf16[128,256]{1,0:T(8,128)(2,1)} copy(bf16[128,256]{1,0:T(8,128)(2,1)} %shard_map.127) | data formatting | bytes 131072
